TPU v7x, 32 devices: a whole 2x2x4 slice. The times are simulated.
32 devices in a mesh: ctx: 8 (over z, x), tp: 4 (over y, core).
Axes of the slice: x: 2, y: 2, z: 4, core: 2. Of those that a mesh axis runs over, the one named last changes fastest.
Arguments:
- hidden_in: bfloat16 [2048, 3072], P('ctx', 'tp'), may hold values from -96 to 96
- norm_gain: float32 [3072], replicated, may hold values from 0.1 to 1.9
- w_query: bfloat16 [3072, 3072], P(None, 'tp'), may hold values from -1 to 1
- w_key: bfloat16 [3072, 3072], P(None, 'tp'), may hold values from -1 to 1
- w_value: bfloat16 [3072, 3072], P(None, 'tp'), may hold values from -0.109375 to 0.109375
- w_out: bfloat16 [3072, 3072], P('tp'), may hold values from -0.109375 to 0.109375
- head_gain: float32 [3072], replicated, may hold values from 0.1 to 1.9
- proj_head: bfloat16 [3072, 2048], P('tp'), may hold values from -0.109375 to 0.109375
- proj_middle: bfloat16 [3072, 512], P('tp'), may hold values from -0.109375 to 0.109375
- proj_tail: bfloat16 [3072, 128], P('tp'), may hold values from -0.109375 to 0.109375
- table_head: bfloat16 [10240, 2048], P(('tp', 'ctx')), may hold values from -64 to 64
- table_middle: bfloat16 [20480, 512], P(('tp', 'ctx')), may hold values from -64 to 64
- table_tail: bfloat16 [104448, 128], P(('tp', 'ctx')), may hold values from -64 to 64
- clusters: bfloat16 [2, 2048], replicated, may hold values from -0.375 to 0.375
- targets: int32 [2048], P('ctx'), may hold values from 0 to 135167
Outputs:
- hidden_out: bfloat16 [2048, 3072], P('ctx', 'tp')
- losses: float32 [2048], P('ctx')
All inputs are finite; a program needn't handle non-finite values.
Results may differ from a plain program's by a relative error of at most 0.004.
Values may be sent and summed in bfloat16 or wider, within the bound.
A program may use at most 128 MiB of HBM per device.

v0:
```python
import jax
import jax.numpy as jnp
from jax import lax
from jax.sharding import PartitionSpec as P

D = 3072
HD = 96
V0 = 10240
V1 = 20480


NEG_FILL = -1e30


def passed_along(block, axis, distance):
    devices = range(lax.axis_size(axis))
    route = [(i - distance, i) for i in devices if i - distance in devices]
    return lax.ppermute(block, axis, route)


def merged(part, axis, combine):
    gathered = jax.tree.map(lambda a: lax.all_gather(a, axis), part)

    def take(source):
        return jax.tree.map(lambda a: lax.dynamic_index_in_dim(a, source, 0, False), gathered)

    return lax.fori_loop(
        1, lax.axis_size(axis), lambda source, state: combine(state, take(source)), take(0)
    )


def merge_stats(first_stats, second_stats):
    top_value = jnp.maximum(first_stats[0], second_stats[0])
    sum_exp = first_stats[1] * jnp.exp(first_stats[0] - top_value) + second_stats[1] * jnp.exp(
        second_stats[0] - top_value
    )
    return (top_value, sum_exp, first_stats[2] + second_stats[2])


def merge_bands(first_bands, second_bands):
    return tuple(
        (
            merge_stats(one_band, other_band)
            for one_band, other_band in zip(first_bands, second_bands)
        )
    )


def empty_stats(row_total):
    return (
        jnp.full((row_total,), NEG_FILL, jnp.float32),
        jnp.zeros((row_total,), jnp.float32),
        jnp.zeros((row_total,), jnp.float32),
    )


def fold_band(running, table_part, band_rows, local_goal):
    row_count = table_part.shape[0]
    block_rows = min(row_count, 2048)
    for row_start in range(0, row_count, block_rows):
        table_slab = table_part[row_start : row_start + block_rows]
        logits = lax.dot_general(
            table_slab, band_rows, (((1,), (1,)), ((), ())), preferred_element_type=jnp.float32
        )
        word_index = lax.broadcasted_iota(jnp.int32, logits.shape, 0) + row_start
        block_top = jnp.max(logits, 0)
        block_sum = jnp.sum(jnp.exp(logits - block_top[None]), 0)
        block_pick = jnp.sum(jnp.where(word_index == local_goal[None], logits, 0.0), 0)
        running = merge_stats(running, (block_top, block_sum, block_pick))
    return running


def scale_rows(row_values, square_sums, gain_part):
    return (row_values * lax.rsqrt(square_sums / D + 1e-06)[:, None] * gain_part).astype(
        jnp.bfloat16
    )


def project(full_rows, weight):
    return jnp.dot(full_rows, weight, preferred_element_type=jnp.float32).astype(jnp.bfloat16)


def body(
    hidden_in,
    norm_gain,
    w_query,
    w_key,
    w_value,
    w_out,
    head_gain,
    proj_head,
    proj_middle,
    proj_tail,
    table_head,
    table_middle,
    table_tail,
    clusters,
    targets,
):
    seg_len = hidden_in.shape[0]
    local_width = hidden_in.shape[1]
    tp_rank = lax.axis_index("tp")
    ctx_rank = lax.axis_index("ctx")
    ctx_count = lax.axis_size("ctx")
    gain_in = lax.dynamic_slice_in_dim(norm_gain, tp_rank * local_width, local_width)
    gain_out = lax.dynamic_slice_in_dim(head_gain, tp_rank * local_width, local_width)
    own_rows = hidden_in.astype(jnp.float32)
    own_sq = lax.psum(jnp.sum(own_rows * own_rows, 1), "tp")
    own_full = lax.all_gather(scale_rows(own_rows, own_sq, gain_in), "tp", axis=1, tiled=True)
    queries = project(own_full, w_query)
    keys_now = project(own_full, w_key)
    values_now = project(own_full, w_value)
    key_width = keys_now.shape[1]
    carried = passed_along(jnp.concatenate([keys_now, values_now], 1), "ctx", 1)
    memory_keys = carried[:, :key_width]
    memory_values = carried[:, key_width:]
    heads_local = queries.shape[1] // HD
    query_heads = queries.reshape(seg_len, heads_local, HD)
    key_heads = jnp.concatenate([memory_keys, keys_now], 0).reshape(2 * seg_len, heads_local, HD)
    value_heads = jnp.concatenate([memory_values, values_now], 0).reshape(
        2 * seg_len, heads_local, HD
    )
    scores = jnp.einsum(
        "qhe,khe->hqk", query_heads, key_heads, preferred_element_type=jnp.float32
    ) * HD ** (-0.5)
    row_pos = lax.broadcasted_iota(jnp.int32, (seg_len, 2 * seg_len), 0)
    col_pos = lax.broadcasted_iota(jnp.int32, (seg_len, 2 * seg_len), 1)
    allowed = jnp.where(col_pos < seg_len, ctx_rank > 0, col_pos - seg_len <= row_pos)
    scores = jnp.where(allowed[None], scores, NEG_FILL)
    top_score = jnp.max(scores, axis=2, keepdims=True)
    raised = jnp.exp(scores - top_score)
    weights = (raised / jnp.sum(raised, axis=2, keepdims=True)).astype(jnp.bfloat16)
    context = jnp.einsum("hqk,khe->qhe", weights, value_heads, preferred_element_type=jnp.float32)
    context = context.astype(jnp.bfloat16).reshape(seg_len, heads_local * HD)
    partial_out = jnp.dot(context, w_out, preferred_element_type=jnp.float32)
    attention = lax.psum_scatter(
        partial_out.astype(jnp.bfloat16), "tp", scatter_dimension=1, tiled=True
    ).astype(jnp.float32)
    summed = own_rows + attention
    hidden_out = summed.astype(jnp.bfloat16)
    out_sq = lax.psum(jnp.sum(summed * summed, 1), "tp")
    normed_out = scale_rows(summed, out_sq, gain_out)
    band_sums = (
        lax.psum(
            jnp.dot(normed_out, proj_head, preferred_element_type=jnp.float32).astype(jnp.bfloat16),
            "tp",
        ).astype(jnp.float32),
        lax.psum(
            jnp.dot(normed_out, proj_middle, preferred_element_type=jnp.float32).astype(
                jnp.bfloat16
            ),
            "tp",
        ).astype(jnp.float32),
        lax.psum(
            jnp.dot(normed_out, proj_tail, preferred_element_type=jnp.float32).astype(jnp.bfloat16),
            "tp",
        ).astype(jnp.float32),
    )
    inputs_head = band_sums[0].astype(jnp.bfloat16)
    inputs_middle = band_sums[1].astype(jnp.bfloat16)
    inputs_tail = band_sums[2].astype(jnp.bfloat16)
    rows_head = table_head.shape[0]
    rows_middle = table_middle.shape[0]
    rows_tail = table_tail.shape[0]
    head_base = tp_rank * rows_head * ctx_count
    head_stats = fold_band(
        empty_stats(seg_len),
        lax.all_gather(table_head, "ctx", axis=0, tiled=True),
        inputs_head,
        targets - head_base,
    )
    middle_base = tp_rank * rows_middle * ctx_count
    tail_base = tp_rank * rows_tail * ctx_count
    middle_stats = fold_band(
        empty_stats(seg_len),
        lax.all_gather(table_middle, "ctx", axis=0, tiled=True),
        inputs_middle,
        targets - V0 - middle_base,
    )
    tail_stats = fold_band(
        empty_stats(seg_len),
        lax.all_gather(table_tail, "ctx", axis=0, tiled=True),
        inputs_tail,
        targets - V0 - V1 - tail_base,
    )
    head_stats, middle_stats, tail_stats = merged(
        (head_stats, middle_stats, tail_stats), "tp", merge_bands
    )
    word_total = head_stats[0] + jnp.log(head_stats[1])
    cluster_logits = lax.dot_general(
        inputs_head, clusters, (((1,), (1,)), ((), ())), preferred_element_type=jnp.float32
    )
    first_cluster = cluster_logits[:, 0]
    second_cluster = cluster_logits[:, 1]
    highest = jnp.maximum(word_total, jnp.maximum(first_cluster, second_cluster))
    head_total = highest + jnp.log(
        jnp.exp(word_total - highest)
        + jnp.exp(first_cluster - highest)
        + jnp.exp(second_cluster - highest)
    )
    middle_total = middle_stats[0] + jnp.log(middle_stats[1])
    tail_total = tail_stats[0] + jnp.log(tail_stats[1])
    loss_head = head_total - head_stats[2]
    loss_middle = head_total - first_cluster + middle_total - middle_stats[2]
    loss_tail = head_total - second_cluster + tail_total - tail_stats[2]
    losses = jnp.where(
        targets < V0, loss_head, jnp.where(targets < V0 + V1, loss_middle, loss_tail)
    )
    return (hidden_out, losses)


def solution(mesh):
    placed = (
        P("ctx", "tp"),
        P(),
        P(None, "tp"),
        P(None, "tp"),
        P(None, "tp"),
        P("tp", None),
        P(),
        P("tp", None),
        P("tp", None),
        P("tp", None),
        P(("tp", "ctx"), None),
        P(("tp", "ctx"), None),
        P(("tp", "ctx"), None),
        P(),
        P("ctx"),
    )
    return jax.shard_map(
        body, mesh=mesh, in_specs=placed, out_specs=(P("ctx", "tp"), P("ctx")), check_vma=False
    )
```

profile of v0, /device:TPU:0, one launch (start us, length us, event | category | flops | bytes accessed | tf_op | source)
XLA Modules:
  0.0 512.6 jit_solution(7919128031519480269)
XLA Ops:
  8.1 1.3 fusion.68
  9.4 8.4 %psum.35 = f32[256]{0:T(256)S(1)} all-reduce(f32[256]{0:T(256)S(1)} %fusion.68), channel_id=1, replica_groups=mesh['ctx'=8,'tp'=4] {'tp'}, use_global_device_ids=true, to_apply=%region_1.0 | all-reduce | flops 256 | bytes 2048 | tf_op jit(solution)/shard_map/psum | solution.py:108
  18.5 1.9 fusion.70
  20.5 20.0 %all-gather.16.cloned.1.call-done = bf16[256,3072]{1,0:T(8,128)(2,1)} async-done(((bf16[256,768]{1,0:T(8,128)(2,1)}), bf16[256,3072]{1,0:T(8,128)(2,1)}) %all-gather.16.cloned.1.call-update) | async-done | bytes 1572880 | tf_op jit(solution)/shard_map/all_gather | solution.py:109
  40.6 4.3 convolution_convert_fusion.3
  44.9 3.8 convolution_convert_fusion.4
  50.4 4.3 collective-permute-start
  55.4 2.2 convolution_convert_fusion.2
  57.6 1.9 copy.24
  59.5 11.8 %collective-permute-done = bf16[256,1536]{1,0:T(8,128)(2,1)} collective-permute-done((bf16[256,1536]{1,0:T(8,128)(2,1)}, bf16[256,1536]{1,0:T(8,128)(2,1)}, u32[]{:S(2)}, u32[]{:S(2)}) %collective-permute-start) | collective-permute-done | bytes 786464 | tf_op jit(solution)/shard_map/ppermute | solution.py:18
  71.3 1.2 fusion.106
  72.4 2.3 pad_maximum_fusion.1
  74.7 2.3 copy.25
  77.0 2.3 copy.23
  79.4 4.7 fusion.108
  84.0 3.3 fusion.62
  87.4 5.0 convolution_convert_fusion
  93.2 28.5 %reduce-scatter.2.cloned.1.call-done = bf16[256,768]{1,0:T(8,128)(2,1)} async-done(((bf16[256,3072]{1,0:T(8,128)(2,1)}), bf16[256,768]{1,0:T(8,128)(2,1)}) %reduce-scatter.2.cloned.1.call-update) | async-done | bytes 393232 | tf_op jit(solution)/shard_map/reduce_scatter | solution.py:136
  121.7 1.2 multiply_reduce_fusion
  122.9 5.8 %psum.36 = f32[256]{0:T(256)S(1)} all-reduce(f32[256]{0:T(256)S(1)} %multiply_reduce_fusion), channel_id=1, replica_groups=mesh['ctx'=8,'tp'=4] {'tp'}, use_global_device_ids=true, to_apply=%region_6.7 | all-reduce | flops 256 | bytes 2048 | tf_op jit(solution)/shard_map/psum | solution.py:141
  128.6 1.9 multiply_convert_fusion
  130.6 2.0 convolution_convert_fusion.1
  132.5 1.1 convolution_convert_fusion.5
  136.4 39.6 %all-reduce.3.cloned.1.call-done = (bf16[256,2048]{1,0:T(8,128)(2,1)}, bf16[256,512]{1,0:T(8,128)(2,1)}, bf16[256,128]{1,0:T(8,128)(2,1)}) async-done(((bf16[256,2048]{1,0:T(8,128)(2,1)}, bf16[256,512]{1,0:T(8,128)(2,1)}, bf16[256,128]{1,0:T(8,128)(2,1)}), (bf16[256,2048]{1,0:T(8,128)(2,1)}, bf16[256,512]{1,0:T(8,128)(2,1)}, bf16[256,128]{1,0:T(8,128)(2,1)})) %all-reduce.3.cloned.1.call-update) | async-done | bytes 1376272 | tf_op jit(solution)/shard_map/psum | solution.py:144
  175.9 1.9 fusion.127
  177.8 46.4 %all-gather.20.cloned.1.call-done = bf16[5120,512]{1,0:T(8,128)(2,1)} async-done(((bf16[640,512]{1,0:T(8,128)(2,1)}), bf16[5120,512]{1,0:T(8,128)(2,1)}) %all-gather.20.cloned.1.call-update) | async-done | bytes 5242896 | tf_op jit(solution)/shard_map/all_gather | solution.py:176
  224.2 1.9 fusion.111
  226.5 3.7 fusion.113
  230.2 3.9 fusion.114
  234.1 93.9 %all-gather.22.cloned.1.call-done = bf16[26112,128]{1,0:T(8,128)(2,1)} async-done(((bf16[3264,128]{1,0:T(8,128)(2,1)}), bf16[26112,128]{1,0:T(8,128)(2,1)}) %all-gather.22.cloned.1.call-update) | async-done | bytes 6684688 | tf_op jit(solution)/shard_map/all_gather | solution.py:182
  328.0 1.4 fusion.118
  330.0 1.8 fusion.121
  331.8 1.6 fusion.122
  338.6 1.2 fusion.15
  339.7 3.6 fusion.45
  343.4 3.4 fusion.42
  346.9 5.1 all-gather.10
  352.0 5.1 all-gather.9
  357.1 5.1 all-gather.8
  362.2 5.1 all-gather.7
  367.2 5.1 all-gather.5
  372.3 5.1 all-gather.6
  377.4 101.4 %all-gather.18.cloned.1.call-done = bf16[2560,2048]{1,0:T(8,128)(2,1)} async-done(((bf16[320,2048]{1,0:T(8,128)(2,1)}), bf16[2560,2048]{1,0:T(8,128)(2,1)}) %all-gather.18.cloned.1.call-update) | async-done | bytes 10485776 | tf_op jit(solution)/shard_map/all_gather | solution.py:168
  478.8 5.8 %fusion.110 = (f32[256]{0:T(256)S(1)}, f32[256,2048]{1,0:T(8,128)S(1)}) fusion(bf16[256,2048]{1,0:T(8,128)(2,1)S(1)} %copy-done.9, bf16[2560,2048]{1,0:T(8,128)(2,1)} %all-gather.18.cloned.1.call-done), kind=kOutput, calls=%fused_computation.219 | convolution fusion | flops 2148007680 | bytes 11535360 | tf_op jit(solution)/shard_map/dot_general | solution.py:62
  486.0 2.5 fusion.109
  488.7 5.1 all-gather.4
  493.8 5.1 all-gather.2
  498.9 5.1 all-gather.3
  (163 shorter events, 16.4 us)
Async XLA Ops:
  8.0 122.6 %copy-start = (bf16[768,2048]{1,0:T(8,128)(2,1)S(1)}, bf16[768,2048]{1,0:T(8,128)(2,1)}, u32[]{:S(2)}) copy-start(bf16[768,2048]{1,0:T(8,128)(2,1)} %param.24) | copy-start | bytes 9437188
  8.0 32.5 %all-gather.16.cloned.1.call-start = ((), (), s32[]{:S(2)}) async-start(), calls=%async_computation.1 | async-start | bytes 1966080 | tf_op jit(solution)/shard_map/all_gather | solution.py:109
  20.4 101.2 %reduce-scatter.2.cloned.1.call-start = ((), (), s32[]{:S(2)}) async-start(), calls=%async_computation.2 | async-start | bytes 1966080 | tf_op jit(solution)/shard_map/reduce_scatter | solution.py:136
  40.6 4.3 copy-start.22
  40.6 14.9 %slice-start.6 = ((s8[4718592]{0:T(1024)(128)(4,1)}), s8[4194304]{0:T(1024)(128)(4,1)S(1)}, s32[]{:S(2)}) async-start(s8[4718592]{0:T(1024)(128)(4,1)} %bitcast.408), calls=%async_computation.13 | async-start | bytes 8388608
  44.9 10.5 %slice-start.7 = ((s8[4718592]{0:T(1024)(128)(4,1)}), s8[524288]{0:T(1024)(128)(4,1)S(1)}, s32[]{:S(2)}) async-start(s8[4718592]{0:T(1024)(128)(4,1)} %bitcast.408), calls=%async_computation.14 | async-start | bytes 1048576
  48.7 0.7 copy-start.8
  50.4 20.9 %collective-permute-start = (bf16[256,1536]{1,0:T(8,128)(2,1)}, bf16[256,1536]{1,0:T(8,128)(2,1)}, u32[]{:S(2)}, u32[]{:S(2)}) collective-permute-start(bf16[256,1536]{1,0:T(8,128)(2,1)} %pad_maximum_fusion), channel_id=1, source_target_pairs={{0,4},{4,8},{8,12},{12,16},{16,20},{20,24},{24,28},{1,5},{5,9},{9,... | collective-permute-start | bytes 2359304 | tf_op jit(solution)/shard_map/ppermute | solution.py:18
  74.7 4.7 copy-start.12
  87.4 34.3 %copy-start.6 = (bf16[256,768]{1,0:T(8,128)(2,1)S(1)}, bf16[256,768]{1,0:T(8,128)(2,1)}, u32[]{:S(2)}) copy-start(bf16[256,768]{1,0:T(8,128)(2,1)} %param.17) | copy-start | bytes 1179652
  92.4 83.6 %all-reduce.3.cloned.1.call-start = ((), (), s32[]{:S(2)}) async-start(), calls=%async_computation.6 | async-start | bytes 2752512 | tf_op jit(solution)/shard_map/psum | solution.py:144
  130.5 2.0 copy-start.11
  130.6 3.1 copy-start.13
  134.5 1.9 copy-start.21
  134.5 41.5 %copy-start.20 = (bf16[2,2048]{1,0:T(2,128)(2,1)S(1)}, bf16[2,2048]{1,0:T(2,128)(2,1)}, u32[]{:S(2)}) copy-start(bf16[2,2048]{1,0:T(2,128)(2,1)} %param.30) | copy-start | bytes 24580
  134.5 89.7 %all-gather.20.cloned.1.call-start = ((), (), s32[]{:S(2)}) async-start(), calls=%async_computation.4 | async-start | bytes 5898240 | tf_op jit(solution)/shard_map/all_gather | solution.py:176
  135.1 192.9 %all-gather.22.cloned.1.call-start = ((), (), s32[]{:S(2)}) async-start(), calls=%async_computation.5 | async-start | bytes 7520256 | tf_op jit(solution)/shard_map/all_gather | solution.py:182
  135.7 343.1 %all-gather.18.cloned.1.call-start = ((), (), s32[]{:S(2)}) async-start(), calls=%async_computation.3 | async-start | bytes 11796480 | tf_op jit(solution)/shard_map/all_gather | solution.py:168
  175.9 50.6 %copy-start.7 = (bf16[256,512]{1,0:T(8,128)(2,1)S(1)}, bf16[256,512]{1,0:T(8,128)(2,1)}, u32[]{:S(2)}) copy-start(bf16[256,512]{1,0:T(8,128)(2,1)} %get-tuple-element.556) | copy-start | bytes 786436
  230.2 97.8 %copy-start.2 = (bf16[256,128]{1,0:T(8,128)(2,1)S(1)}, bf16[256,128]{1,0:T(8,128)(2,1)}, u32[]{:S(2)}) copy-start(bf16[256,128]{1,0:T(8,128)(2,1)} %get-tuple-element.557) | copy-start | bytes 196612
  329.4 3.9 copy-start.5
  339.7 3.6 copy-start.3
  339.7 3.6 copy-start.4
  343.4 135.4 %copy-start.9 = (bf16[256,2048]{1,0:T(8,128)(2,1)S(1)}, bf16[256,2048]{1,0:T(8,128)(2,1)}, u32[]{:S(2)}) copy-start(bf16[256,2048]{1,0:T(8,128)(2,1)} %get-tuple-element.555) | copy-start | bytes 3145732
  351.9 132.7 %copy-start.14 = (f32[4,1,256]{2,1,0:T(1,128)}, f32[4,1,256]{2,1,0:T(1,128)S(1)}, u32[]{:S(2)}) copy-start(f32[4,1,256]{2,1,0:T(1,128)S(1)} %all-gather.10) | copy-start | bytes 12292
  357.1 127.6 %copy-start.16 = (f32[4,1,256]{2,1,0:T(1,128)}, f32[4,1,256]{2,1,0:T(1,128)S(1)}, u32[]{:S(2)}) copy-start(f32[4,1,256]{2,1,0:T(1,128)S(1)} %all-gather.9) | copy-start | bytes 12292
  362.2 122.5 %copy-start.17 = (f32[4,1,256]{2,1,0:T(1,128)}, f32[4,1,256]{2,1,0:T(1,128)S(1)}, u32[]{:S(2)}) copy-start(f32[4,1,256]{2,1,0:T(1,128)S(1)} %all-gather.8) | copy-start | bytes 12292
  367.2 117.5 %copy-start.15 = (f32[4,1,256]{2,1,0:T(1,128)}, f32[4,1,256]{2,1,0:T(1,128)S(1)}, u32[]{:S(2)}) copy-start(f32[4,1,256]{2,1,0:T(1,128)S(1)} %all-gather.7) | copy-start | bytes 12292
  372.3 112.4 %copy-start.18 = (f32[4,1,256]{2,1,0:T(1,128)}, f32[4,1,256]{2,1,0:T(1,128)S(1)}, u32[]{:S(2)}) copy-start(f32[4,1,256]{2,1,0:T(1,128)S(1)} %all-gather.5) | copy-start | bytes 12292
  377.4 107.3 %copy-start.19 = (f32[4,1,256]{2,1,0:T(1,128)}, f32[4,1,256]{2,1,0:T(1,128)S(1)}, u32[]{:S(2)}) copy-start(f32[4,1,256]{2,1,0:T(1,128)S(1)} %all-gather.6) | copy-start | bytes 12292
  484.7 1.2 copy-start.10
  484.7 20.5 %copy-start.1 = (bf16[768,2048]{1,0:T(8,128)(2,1)S(1)}, bf16[768,2048]{1,0:T(8,128)(2,1)}, u32[]{:S(2)}) copy-start(bf16[768,2048]{1,0:T(8,128)(2,1)} %param.24) | copy-start | bytes 9437188
  485.9 18.0 %slice-start = ((f32[4,1,256]{2,1,0:T(1,128)}), f32[1,1,256]{2,1,0:T(1,128)S(1)}, s32[]{:S(2)}) async-start(f32[4,1,256]{2,1,0:T(1,128)} %copy-done.14), calls=%async_computation.7 | async-start | bytes 2048 | tf_op jit(solution)/shard_map/jit(dynamic_index_in_dim)/dynamic_slice | solution.py:25
  485.9 18.0 %slice-start.1 = ((f32[4,1,256]{2,1,0:T(1,128)}), f32[1,1,256]{2,1,0:T(1,128)S(1)}, s32[]{:S(2)}) async-start(f32[4,1,256]{2,1,0:T(1,128)} %copy-done.15), calls=%async_computation.8 | async-start | bytes 2048 | tf_op jit(solution)/shard_map/jit(dynamic_index_in_dim)/dynamic_slice | solution.py:25
  485.9 18.0 %slice-start.2 = ((f32[4,1,256]{2,1,0:T(1,128)}), f32[1,1,256]{2,1,0:T(1,128)S(1)}, s32[]{:S(2)}) async-start(f32[4,1,256]{2,1,0:T(1,128)} %copy-done.16), calls=%async_computation.9 | async-start | bytes 2048 | tf_op jit(solution)/shard_map/jit(dynamic_index_in_dim)/dynamic_slice | solution.py:25
  485.9 18.0 %slice-start.3 = ((f32[4,1,256]{2,1,0:T(1,128)}), f32[1,1,256]{2,1,0:T(1,128)S(1)}, s32[]{:S(2)}) async-start(f32[4,1,256]{2,1,0:T(1,128)} %copy-done.17), calls=%async_computation.10 | async-start | bytes 2048 | tf_op jit(solution)/shard_map/jit(dynamic_index_in_dim)/dynamic_slice | solution.py:25
  485.9 18.0 %slice-start.4 = ((f32[4,1,256]{2,1,0:T(1,128)}), f32[1,1,256]{2,1,0:T(1,128)S(1)}, s32[]{:S(2)}) async-start(f32[4,1,256]{2,1,0:T(1,128)} %copy-done.18), calls=%async_computation.11 | async-start | bytes 2048 | tf_op jit(solution)/shard_map/jit(dynamic_index_in_dim)/dynamic_slice | solution.py:25
  486.0 18.0 %slice-start.5 = ((f32[4,1,256]{2,1,0:T(1,128)}), f32[1,1,256]{2,1,0:T(1,128)S(1)}, s32[]{:S(2)}) async-start(f32[4,1,256]{2,1,0:T(1,128)} %copy-done.19), calls=%async_computation.12 | async-start | bytes 2048 | tf_op jit(solution)/shard_map/jit(dynamic_index_in_dim)/dynamic_slice | solution.py:25
Sparse Core Ops, SparseCore 0:
  20.6 19.9 all-gather.15
  92.5 29.1 reduce-scatter.1
  134.6 41.2 all-reduce.2
Sparse Core Ops, SparseCore 1:
  137.2 87.0 all-gather.19
  226.3 101.6 all-gather.21
  330.1 148.7 all-gather.17
where the time goes:
time: 513 us
  waiting for transfers between devices  343 us (67%)
  blocking collectives  59.7 us (12%)
  matrix products  56.7 us (11%)
  other arithmetic  21.5 us (4%)
  between operations  15.8 us (3%)
  local copies, waits for them, and re-layouts  10.8 us (2%)
    all_gather x1, waiting for transfers between devices, body(): lax.all_gather(table_head, 'ctx', axis=0, tiled=True)  101 us
    all_gather x1, waiting for transfers between devices, body(): lax.all_gather(table_tail, 'ctx', axis=0, tiled=True)  93.9 us
    all_gather x1, waiting for transfers between devices, body(): lax.all_gather(table_middle, 'ctx', axis=0, tiled=True)  46.4 us
    all_gather x9, blocking collectives, merged(): gathered = jax.tree.map(lambda a: lax.all_gather(a, axis), part)  45.6 us
    psum x1, waiting for transfers between devices, body(): lax.psum(jnp.dot(normed_out, proj_head, preferred_element_type=jnp.float3...  39.6 us
    reduce_scatter x1, waiting for transfers between devices, body(): lax.psum_scatter(partial_out.astype(jnp.bfloat16), 'tp', scatter_dimensio...  28.5 us
    dot_general x18, matrix products, fold_band(): lax.dot_general(table_slab, band_rows, (((1,), (1,)), ((), ())), preferre...  27.7 us
    all_gather x1, waiting for transfers between devices, body(): lax.all_gather(scale_rows(own_rows, own_sq, gain_in), 'tp', axis=1, tiled...  20 us
  transfers between devices with their start and end apart: 7, of which 7 were waited for; matrix products, arithmetic and copies ran while one was open for 7% of the time, Pallas kernels for 0%

commit v1 on v0

v1 whole, which is shorter than its diff:
```python
import jax
import jax.numpy as jnp
from jax import lax
from jax.experimental import pallas as pl
from jax.experimental.pallas import tpu as pltpu
from jax.sharding import PartitionSpec as P

HD = 96
NEG_FILL = -1e30
EPS = 1e-06
F32 = jnp.float32
BF16 = jnp.bfloat16


def norm_full(rows, gain):
    wide = rows.astype(F32)
    mean_sq = jnp.mean(wide * wide, axis=1, keepdims=True)
    return (wide * lax.rsqrt(mean_sq + EPS) * gain[None]).astype(BF16)


def project(full_rows, weight):
    return jnp.dot(full_rows, weight, preferred_element_type=F32).astype(BF16)


def chunk_of(rows):
    best = rows
    if rows > 1024:
        for size in range(16, 1025, 16):
            if rows % size == 0:
                best = size
    return best


def band_stats(band, table_ref, goal):
    rows = table_ref.shape[0]
    chunk = chunk_of(rows)
    top = total = pick = None
    for start in range(0, rows, chunk):
        logits = lax.dot_general(
            table_ref[start : start + chunk, :],
            band,
            (((1,), (1,)), ((), ())),
            preferred_element_type=F32,
        )
        word = lax.broadcasted_iota(jnp.int32, logits.shape, 0)
        chosen = jnp.sum(jnp.where(word == goal - start, logits, 0.0), 0, keepdims=True)
        peak = jnp.max(logits, 0, keepdims=True)
        if top is None:
            top = peak
            total = jnp.sum(jnp.exp(logits - top), 0, keepdims=True)
            pick = chosen
        else:
            higher = jnp.maximum(top, peak)
            total = total * jnp.exp(top - higher) + jnp.sum(
                jnp.exp(logits - higher), 0, keepdims=True
            )
            top = higher
            pick = pick + chosen
    return top, total, pick


def stats_kernel(bands_ref, goals_ref, head_ref, middle_ref, tail_ref, out_ref):
    first = head_ref.shape[1]
    second = first + middle_ref.shape[1]
    one = band_stats(bands_ref[:, :first], head_ref, goals_ref[0:1, :])
    two = band_stats(bands_ref[:, first:second], middle_ref, goals_ref[1:2, :])
    three = band_stats(bands_ref[:, second:], tail_ref, goals_ref[2:3, :])
    out_ref[0:1, :] = one[0]
    out_ref[1:2, :] = one[1]
    out_ref[2:3, :] = two[0]
    out_ref[3:4, :] = two[1]
    out_ref[4:5, :] = three[0]
    out_ref[5:6, :] = three[1]
    out_ref[6:7, :] = one[2] + two[2] + three[2]
    out_ref[7:8, :] = jnp.zeros_like(one[0])


def logit_stats(bands, goals, table_head, table_middle, table_tail):
    tokens, width = bands.shape
    block = 256

    def whole(a):
        return pl.BlockSpec(a.shape, lambda i: (0, 0))

    return pl.pallas_call(
        stats_kernel,
        grid=(tokens // block,),
        in_specs=[
            pl.BlockSpec((block, width), lambda i: (i, 0)),
            pl.BlockSpec((8, block), lambda i: (0, i)),
            whole(table_head),
            whole(table_middle),
            whole(table_tail),
        ],
        out_specs=pl.BlockSpec((8, block), lambda i: (0, i)),
        out_shape=jax.ShapeDtypeStruct((8, tokens), F32),
        compiler_params=pltpu.CompilerParams(vmem_limit_bytes=48 * 1024 * 1024),
    )(bands, goals, table_head, table_middle, table_tail)


def body(
    hidden_in,
    norm_gain,
    w_query,
    w_key,
    w_value,
    w_out,
    head_gain,
    proj_head,
    proj_middle,
    proj_tail,
    table_head,
    table_middle,
    table_tail,
    clusters,
    targets,
):
    seg_len, local_width = hidden_in.shape
    tp_rank = lax.axis_index("tp")
    ctx_rank = lax.axis_index("ctx")
    tp_count = lax.axis_size("tp")
    ctx_count = lax.axis_size("ctx")
    model_width = local_width * tp_count
    v0 = table_head.shape[0] * tp_count * ctx_count
    v1 = table_middle.shape[0] * tp_count * ctx_count

    before = lax.ppermute(hidden_in, "ctx", [(i, i + 1) for i in range(ctx_count - 1)])
    own_full = norm_full(lax.all_gather(hidden_in, "tp", axis=1, tiled=True), norm_gain)
    before_full = norm_full(lax.all_gather(before, "tp", axis=1, tiled=True), norm_gain)
    goals_all = lax.all_gather(targets, "ctx", axis=0, tiled=True)

    queries = project(own_full, w_query)
    keys = jnp.concatenate([project(before_full, w_key), project(own_full, w_key)], 0)
    values = jnp.concatenate([project(before_full, w_value), project(own_full, w_value)], 0)
    heads_local = queries.shape[1] // HD
    query_heads = queries.reshape(seg_len, heads_local, HD)
    key_heads = keys.reshape(2 * seg_len, heads_local, HD)
    value_heads = values.reshape(2 * seg_len, heads_local, HD)
    scores = jnp.einsum(
        "qhe,khe->hqk", query_heads, key_heads, preferred_element_type=F32
    ) * HD ** (-0.5)
    row_pos = lax.broadcasted_iota(jnp.int32, (seg_len, 2 * seg_len), 0)
    col_pos = lax.broadcasted_iota(jnp.int32, (seg_len, 2 * seg_len), 1)
    allowed = jnp.where(col_pos < seg_len, ctx_rank > 0, col_pos - seg_len <= row_pos)
    scores = jnp.where(allowed[None], scores, NEG_FILL)
    top_score = jnp.max(scores, axis=2, keepdims=True)
    raised = jnp.exp(scores - top_score)
    weights = (raised / jnp.sum(raised, axis=2, keepdims=True)).astype(BF16)
    context = jnp.einsum("hqk,khe->qhe", weights, value_heads, preferred_element_type=F32)
    context = context.astype(BF16).reshape(seg_len, heads_local * HD)
    partial_out = jnp.dot(context, w_out, preferred_element_type=F32).astype(BF16)
    attention = lax.psum_scatter(partial_out, "tp", scatter_dimension=1, tiled=True)
    summed = hidden_in.astype(F32) + attention.astype(F32)
    hidden_out = summed.astype(BF16)

    gain_out = lax.dynamic_slice_in_dim(head_gain, tp_rank * local_width, local_width)
    square_sums = lax.psum(jnp.sum(summed * summed, 1), "tp")
    row_scale = lax.rsqrt(square_sums / model_width + EPS)
    scaled = (summed * row_scale[:, None] * gain_out).astype(BF16)
    projection = jnp.concatenate([proj_head, proj_middle, proj_tail], 1)
    partial_bands = jnp.dot(scaled, projection, preferred_element_type=F32).astype(BF16)
    own_bands = lax.psum_scatter(partial_bands, "tp", scatter_dimension=0, tiled=True)
    bands = lax.all_gather(own_bands, ("ctx", "tp"), axis=0, tiled=True)

    place = tp_rank * ctx_count + ctx_rank
    goals = jnp.stack(
        [
            goals_all - place * table_head.shape[0],
            goals_all - v0 - place * table_middle.shape[0],
            goals_all - v0 - v1 - place * table_tail.shape[0],
        ]
        + [jnp.zeros_like(goals_all)] * 5
    )
    stats = logit_stats(bands, goals, table_head, table_middle, table_tail)
    shared = lax.all_to_all(
        stats.reshape(8, ctx_count, seg_len), "ctx", split_axis=1, concat_axis=1, tiled=True
    )
    merged = lax.all_gather(shared, "tp", axis=1, tiled=True)

    def total_of(top, part):
        peak = jnp.max(top, 0)
        return peak + jnp.log(jnp.sum(part * jnp.exp(top - peak[None]), 0))

    head_words = total_of(merged[0], merged[1])
    middle_total = total_of(merged[2], merged[3])
    tail_total = total_of(merged[4], merged[5])
    pick = jnp.sum(merged[6], 0)
    own_rows = lax.dynamic_slice_in_dim(bands, ctx_rank * seg_len, seg_len)
    cluster_logits = lax.dot_general(
        clusters,
        own_rows[:, : clusters.shape[1]],
        (((1,), (1,)), ((), ())),
        preferred_element_type=F32,
    )
    first_cluster, second_cluster = cluster_logits[0], cluster_logits[1]
    highest = jnp.maximum(head_words, jnp.maximum(first_cluster, second_cluster))
    head_total = highest + jnp.log(
        jnp.exp(head_words - highest)
        + jnp.exp(first_cluster - highest)
        + jnp.exp(second_cluster - highest)
    )
    extra = jnp.where(
        targets < v0,
        0.0,
        jnp.where(targets < v0 + v1, middle_total - first_cluster, tail_total - second_cluster),
    )
    return (hidden_out, head_total + extra - pick)


def solution(mesh):
    placed = (
        P("ctx", "tp"),
        P(),
        P(None, "tp"),
        P(None, "tp"),
        P(None, "tp"),
        P("tp", None),
        P(),
        P("tp", None),
        P("tp", None),
        P("tp", None),
        P(("tp", "ctx"), None),
        P(("tp", "ctx"), None),
        P(("tp", "ctx"), None),
        P(),
        P("ctx"),
    )
    return jax.shard_map(
        body, mesh=mesh, in_specs=placed, out_specs=(P("ctx", "tp"), P("ctx")), check_vma=False
    )
```

time: 513 us -> 280 us (0.55)
  waiting for transfers between devices: 343 us -> 157 us
  blocking collectives: 59.7 us -> 32.2 us
  matrix products: 56.7 us -> 36.9 us
  Pallas kernels: 0 us -> 18.9 us
  other arithmetic: 21.5 us -> 7.23 us
  local copies, waits for them, and re-layouts: 10.8 us -> 4.23 us
    all_gather x4 -> x3, waiting for transfers between devices: 262 us -> 86.8 us  [the longest x1 71 us: body(): bands = lax.all_gather(own_bands, ('ctx', 'tp'), axis=0, tiled=True)]
    psum x1 -> x0, waiting for transfers between devices: 39.6 us -> none  [body(): lax.psum(jnp.dot(normed_out, proj_head, preferred_element_type=jnp.float3...]
    reduce_scatter x1 -> x2, waiting for transfers between devices: 28.5 us -> 55.7 us  [the longest x1 28.2 us: body(): lax.psum_scatter(partial_bands, 'tp', scatter_dimension=0, tiled=True)]
    all_gather x9 -> x2, blocking collectives: 45.6 us -> 26.3 us  [the longest x1 20.5 us: body(): goals_all = lax.all_gather(targets, 'ctx', axis=0, tiled=True)]
    pallas_call x0 -> x1, Pallas kernels: none -> 18.9 us  [logit_stats(): pl.pallas_call(stats_kernel, grid=(tokens // block,), in_specs=[pl.BlockS...]
    dot_general x27 -> x9, matrix products: 52 us -> 33.3 us  [the longest x5 21 us: project(): return jnp.dot(full_rows, weight, preferred_element_type=F32).astype(BF16)]
    psum x2 -> x1, blocking collectives: 14.1 us -> 5.91 us  [body(): square_sums = lax.psum(jnp.sum(summed * summed, 1), 'tp')]
    reduce_sum x9 -> x5, other arithmetic: 12.7 us -> 5.54 us  [the longest x2 3.59 us: norm_full(): mean_sq = jnp.mean(wide * wide, axis=1, keepdims=True)]
  transfers between devices with their start and end apart: 7 -> 7, of which waited for: 7 -> 7; matrix products, arithmetic and copies ran while one was open for 7% -> 6% of each run, Pallas kernels for 0% -> 0%
where the time goes in v1:
time: 280 us
  waiting for transfers between devices  157 us (56%)
  matrix products  36.9 us (13%)
  blocking collectives  32.2 us (12%)
  Pallas kernels  18.9 us (7%)
  between operations  14 us (5%)
  starting transfers between devices  8.96 us (3%)
  other arithmetic  7.23 us (3%)
  local copies, waits for them, and re-layouts  4.23 us (2%)
    all_gather x1, waiting for transfers between devices, body(): bands = lax.all_gather(own_bands, ('ctx', 'tp'), axis=0, tiled=True)  71 us
    reduce_scatter x1, waiting for transfers between devices, body(): lax.psum_scatter(partial_bands, 'tp', scatter_dimension=0, tiled=True)  28.2 us
    reduce_scatter x1, waiting for transfers between devices, body(): lax.psum_scatter(partial_out, 'tp', scatter_dimension=1, tiled=True)  27.5 us
    dot_general x5, matrix products, project(): return jnp.dot(full_rows, weight, preferred_element_type=F32).astype(BF16)  21 us
    all_gather x1, blocking collectives, body(): goals_all = lax.all_gather(targets, 'ctx', axis=0, tiled=True)  20.5 us
    pallas_call x1, Pallas kernels, logit_stats(): pl.pallas_call(stats_kernel, grid=(tokens // block,), in_specs=[pl.BlockS...  18.9 us
    all_gather x1, waiting for transfers between devices, body(): lax.all_gather(hidden_in, 'tp', axis=1, tiled=True)  8.9 us
    ppermute x1, waiting for transfers between devices, body(): lax.ppermute(hidden_in, 'ctx', [(i, i + 1) for i in range(ctx_count - 1)])  8.64 us
  transfers between devices with their start and end apart: 7, of which 7 were waited for; matrix products, arithmetic and copies ran while one was open for 6% of the time, Pallas kernels for 0%

profile of v1, /device:TPU:0, one launch (start us, length us, event | category | flops | bytes accessed | tf_op | source)
XLA Modules:
  0.0 279.6 jit_solution(11713081000225525698)
XLA Ops:
  7.2 0.0 all-gather.7.cloned.1.call-start
  7.2 0.7 all-gather.7.cloned.1.call-update
  7.9 0.0 all-gather.5.cloned.1.call-start
  8.0 4.9 %collective-permute-start = (bf16[256,768]{1,0:T(8,128)(2,1)}, bf16[256,768]{1,0:T(8,128)(2,1)S(1)}, u32[]{:S(2)}, u32[]{:S(2)}) collective-permute-start(bf16[256,768]{1,0:T(8,128)(2,1)} %param.15), channel_id=1, source_target_pairs={{0,4},{4,8},{8,12},{12,16},{16,20},{20,24},{24,28},{1,5},{5,9},{9,... | collective-permute-start | bytes 1179656 | tf_op jit(solution)/shard_map/ppermute | solution.py:127
  12.8 8.6 %collective-permute-done = bf16[256,768]{1,0:T(8,128)(2,1)S(1)} collective-permute-done((bf16[256,768]{1,0:T(8,128)(2,1)}, bf16[256,768]{1,0:T(8,128)(2,1)S(1)}, u32[]{:S(2)}, u32[]{:S(2)}) %collective-permute-start) | collective-permute-done | bytes 393248 | tf_op jit(solution)/shard_map/ppermute | solution.py:127
  21.5 0.7 copy-done.7
  22.2 0.0 all-gather.5.cloned.1.call-update
  22.3 0.0 reduce-scatter.3.cloned.1.call-start
  22.3 0.7 fusion.24
  23.1 8.9 %all-gather.7.cloned.1.call-done = bf16[256,3072]{1,0:T(8,128)(2,1)} async-done(((bf16[256,768]{1,0:T(8,128)(2,1)}), bf16[256,3072]{1,0:T(8,128)(2,1)}) %all-gather.7.cloned.1.call-update) | async-done | bytes 1572880 | tf_op jit(solution)/shard_map/all_gather | solution.py:128
  32.0 1.8 fusion.14
  33.8 4.4 %convolution_convert_fusion.3 = bf16[256,768]{1,0:T(8,128)(2,1)S(1)} fusion(bf16[3072,768]{1,0:T(8,128)(2,1)} %param.17, bf16[256,3072]{1,0:T(8,128)(2,1)} %all-gather.7.cloned.1.call-done, f32[256]{0:T(256)S(1)} %add_rsqrt_fusion.1, f32[3072]{0:T(1024)} %param.16), kind=kOutput, calls=%fused_computation.30 | convolution fusion | flops 1211301888 | bytes 6697984 | tf_op jit(solution)/shard_map/dot_general | solution.py:22
  38.2 0.2 copy.30
  38.4 4.7 %convolution_convert_fusion.1 = bf16[256,768]{1,0:T(8,128)(2,1)} fusion(bf16[3072,768]{1,0:T(8,128)(2,1)} %param.18, bf16[256,3072]{1,0:T(8,128)(2,1)S(1)} %copy-done.4, f32[256]{0:T(256)S(1)} %add_rsqrt_fusion.1, f32[3072]{0:T(1024)S(1)} %copy-done.12), kind=kOutput, calls=%fused_computation.28 | convolution fusion | flops 1211301888 | bytes 6697984 | tf_op jit(solution)/shard_map/dot_general | solution.py:22
  43.1 3.8 %convolution_convert_fusion.4 = bf16[256,768]{1,0:T(8,128)(2,1)S(1)} fusion(bf16[3072,768]{1,0:T(8,128)(2,1)} %param.19, bf16[256,3072]{1,0:T(8,128)(2,1)S(1)} %copy-done.4, f32[256]{0:T(256)S(1)} %add_rsqrt_fusion.1, f32[3072]{0:T(1024)S(1)} %copy-done.12), kind=kOutput, calls=%fused_computation.31 | convolution fusion | flops 1211301888 | bytes 6697984 | tf_op jit(solution)/shard_map/dot_general | solution.py:22
  46.9 6.9 %all-gather.5.cloned.1.call-done = bf16[256,3072]{1,0:T(8,128)(2,1)} async-done(((bf16[256,768]{1,0:T(8,128)(2,1)}), bf16[256,3072]{1,0:T(8,128)(2,1)}) %all-gather.5.cloned.1.call-update) | async-done | bytes 1572880 | tf_op jit(solution)/shard_map/all_gather | solution.py:129
  53.8 1.8 fusion.11
  55.6 4.3 %convolution_convert_fusion.5 = bf16[256,768]{1,0:T(8,128)(2,1)S(1)} fusion(bf16[3072,768]{1,0:T(8,128)(2,1)} %param.19, bf16[256,3072]{1,0:T(8,128)(2,1)} %all-gather.5.cloned.1.call-done, f32[3072]{0:T(1024)S(1)} %copy-done.12, f32[256]{0:T(256)S(1)} %add_rsqrt_fusion.2), kind=kOutput, calls=%fused_computation.32 | convolution fusion | flops 1211301888 | bytes 6697984 | tf_op jit(solution)/shard_map/dot_general | solution.py:22
  59.9 0.1 pad_maximum_fusion
  59.9 0.3 copy.29
  60.2 1.1 copy-done.5
  61.3 3.9 %convolution_convert_fusion.2 = bf16[256,768]{1,0:T(8,128)(2,1)S(1)} fusion(bf16[3072,768]{1,0:T(8,128)(2,1)} %param.18, bf16[256,3072]{1,0:T(8,128)(2,1)S(1)} %copy-done.5, f32[3072]{0:T(1024)} %param.16, f32[256]{0:T(256)S(1)} %add_rsqrt_fusion.2), kind=kOutput, calls=%fused_computation.29 | convolution fusion | flops 1211301888 | bytes 6697984 | tf_op jit(solution)/shard_map/dot_general | solution.py:22
  65.2 0.1 pad_maximum_fusion.1
  65.3 0.3 copy.31
  65.5 0.5 copy-done.9
  66.1 3.6 %fusion.54 = (f32[8,256]{1,0:T(8,128)S(1)}, f32[8,256,512]{2,1,0:T(8,128)}) fusion(pred[256,512]{1,0:T(8,128)(4,1)S(1)} %copy-done.9, bf16[256,8,96]{0,2,1:T(8,128)(2,1)S(1)} %bitcast.69, bf16[512,8,96]{0,2,1:T(8,128)(2,1)S(1)} %bitcast.68), kind=kOutput, calls=%fused_computation.83 | convolution fusion | flops 205521408 | bytes 5513216 | tf_op jit(solution)/shard_map/sub | solution.py:147
  69.6 3.2 %fusion.21 = bf16[8,96,256]{2,1,0:T(8,128)(2,1)S(1)} fusion(bf16[512,8,96]{0,2,1:T(8,128)(2,1)S(1)} %bitcast.67, f32[8,256,512]{2,1,0:T(8,128)} %get-tuple-element.24, f32[8,256]{1,0:T(8,128)S(1)} %get-tuple-element.23), kind=kOutput, calls=%fused_computation.27 | convolution fusion | flops 203620352 | bytes 5382144 | tf_op jit(solution)/shard_map/hqk,khe->qhe/dot_general | solution.py:149
  72.9 0.2 slice-done.1
  73.1 2.6 convolution_convert_fusion
  75.7 0.0 reduce-scatter.5.cloned.1.call-start
  75.8 0.8 dynamic_slice.6
  76.6 27.5 %reduce-scatter.3.cloned.1.call-done = bf16[256,768]{1,0:T(8,128)(2,1)} async-done(((bf16[256,3072]{1,0:T(8,128)(2,1)}), bf16[256,768]{1,0:T(8,128)(2,1)}) %reduce-scatter.3.cloned.1.call-update) | async-done | bytes 393232 | tf_op jit(solution)/shard_map/reduce_scatter | solution.py:152
  104.1 1.9 multiply_reduce_fusion
  105.9 5.9 %psum.7 = f32[256]{0:T(256)S(1)} all-reduce(f32[256]{0:T(256)S(1)} %get-tuple-element.6), channel_id=1, replica_groups=mesh['ctx'=8,'tp'=4] {'tp'}, use_global_device_ids=true, to_apply=%region_6.7 | all-reduce | flops 256 | bytes 2048 | tf_op jit(solution)/shard_map/psum | solution.py:157
  111.9 4.9 %fusion.7 = bf16[256,2688]{1,0:T(8,128)(2,1)} fusion(bf16[768,128]{1,0:T(8,128)(2,1)S(1)} %copy-done.11, bf16[768,512]{1,0:T(8,128)(2,1)} %param.23, bf16[768,2048]{1,0:T(8,128)(2,1)} %param.22, bf16[256,768]{1,0:T(8,128)(2,1)} %reduce-scatter.3.cloned.1.call-done, bf16[256,768]{1,0:T(8,128)(2,1)S(1)} %copy-done.6, f32[768]{0:T(1024)S(1)} %dynamic_slice.6, ...), kind=kOutput, calls=%fused_computation.14 | convolution fusion | flops 1071218688 | bytes 6295552 | tf_op jit(solution)/shard_map/dot_general | solution.py:161
  116.8 0.0 all-gather.9.cloned.1.call-start
  116.9 28.2 %reduce-scatter.5.cloned.1.call-done = bf16[64,2688]{1,0:T(8,128)(2,1)} async-done(((bf16[256,2688]{1,0:T(8,128)(2,1)}), bf16[64,2688]{1,0:T(8,128)(2,1)}) %reduce-scatter.5.cloned.1.call-update) | async-done | bytes 344080 | tf_op jit(solution)/shard_map/reduce_scatter | solution.py:162
  145.0 0.0 all-gather.9.cloned.1.call-update
  145.1 20.5 %all-gather = s32[8,1,256]{2,1,0:T(1,128)S(1)} all-gather(s32[1,1,256]{2,1,0:T(1,128)S(1)} %bitcast.73), channel_id=1, replica_groups=mesh['ctx'=8,'tp'=4] {'ctx'}, dimensions={0}, use_global_device_ids=true | all-gather | bytes 9216 | tf_op jit(solution)/shard_map/all_gather | solution.py:130
  165.7 0.1 stack.19.goals_ref
  165.7 71.0 %all-gather.9.cloned.1.call-done.bands_ref = bf16[2048,2688]{1,0:T(8,128)(2,1)} async-done(((bf16[64,2688]{1,0:T(8,128)(2,1)}), bf16[2048,2688]{1,0:T(8,128)(2,1)}) %all-gather.9.cloned.1.call-update) | async-done | bytes 11010064 | tf_op jit(solution)/shard_map/all_gather | solution.py:163
  236.7 18.9 %shard_map.158 = f32[8,2048]{1,0:T(8,128)} custom-call(bf16[2048,2688]{1,0:T(8,128)(2,1)} %all-gather.9.cloned.1.call-done.bands_ref, s32[8,2048]{1,0:T(8,128)S(1)} %stack.19.goals_ref, bf16[320,2048]{1,0:T(8,128)(2,1)S(1)} %copy-done.1, bf16[640,512]{1,0:T(8,128)(2,1)S(1)} %copy-done.3, bf16[3264,128]{1,0:T(8,128)(2,1)S(1)} %copy-done.2), custom_call_target="tpu_custom_call" | custom-call | tf_op jit(solution)/shard_map/pallas_call | solution.py:85
  255.7 3.9 %all-to-all-start = ((f32[8,8,256]{2,0,1:T(8,128)}), f32[8,8,256]{2,0,1:T(8,128)S(1)}, u32[]{:S(2)}, u32[]{:S(2)}) async-start(f32[8,8,256]{2,0,1:T(8,128)} %bitcast.9), calls=%async_computation.2 | async-start | bytes 131072 | tf_op jit(solution)/shard_map/all_to_all | solution.py:175
  259.6 1.6 convolution_bitcast_fusion
  261.2 5.3 %all-to-all-done = f32[8,8,256]{2,0,1:T(8,128)S(1)} async-done(((f32[8,8,256]{2,0,1:T(8,128)}), f32[8,8,256]{2,0,1:T(8,128)S(1)}, u32[]{:S(2)}, u32[]{:S(2)}) %all-to-all-start) | async-done | bytes 65568 | tf_op jit(solution)/shard_map/all_to_all | solution.py:175
  266.5 5.8 %all_gather.19 = f32[8,32,256]{2,0,1:T(8,128)S(1)} all-gather(f32[8,8,256]{2,0,1:T(8,128)S(1)} %all-to-all-done), channel_id=1, replica_groups=mesh['ctx'=8,'tp'=4] {'tp'}, dimensions={1}, use_global_device_ids=true | all-gather | bytes 327680 | tf_op jit(solution)/shard_map/all_gather | solution.py:178
  272.2 0.2 fusion.52
  272.5 0.6 fusion.44
  (40 shorter events, 0.2 us)
Async XLA Ops:
  7.2 252.4 %copy-start = (bf16[2,2048]{1,0:T(2,128)(2,1)S(1)}, bf16[2,2048]{1,0:T(2,128)(2,1)}, u32[]{:S(2)}) copy-start(bf16[2,2048]{1,0:T(2,128)(2,1)} %param.28) | copy-start | bytes 24580
  7.2 24.8 %all-gather.7.cloned.1.call-start = ((), (), s32[]{:S(2)}) async-start(), calls=%async_computation.4 | async-start | bytes 1966080 | tf_op jit(solution)/shard_map/all_gather | solution.py:128
  7.9 45.9 %all-gather.5.cloned.1.call-start = ((), (), s32[]{:S(2)}) async-start(), calls=%async_computation.3 | async-start | bytes 1966080 | tf_op jit(solution)/shard_map/all_gather | solution.py:129
  8.0 13.5 %collective-permute-start = (bf16[256,768]{1,0:T(8,128)(2,1)}, bf16[256,768]{1,0:T(8,128)(2,1)S(1)}, u32[]{:S(2)}, u32[]{:S(2)}) collective-permute-start(bf16[256,768]{1,0:T(8,128)(2,1)} %param.15), channel_id=1, source_target_pairs={{0,4},{4,8},{8,12},{12,16},{16,20},{20,24},{24,28},{1,5},{5,9},{9,... | collective-permute-start | bytes 1179656 | tf_op jit(solution)/shard_map/ppermute | solution.py:127
  21.5 0.7 copy-start.7
  22.3 81.8 %reduce-scatter.3.cloned.1.call-start = ((), (), s32[]{:S(2)}) async-start(), calls=%async_computation.5 | async-start | bytes 1966080 | tf_op jit(solution)/shard_map/reduce_scatter | solution.py:152
  33.8 4.6 %copy-start.4 = (bf16[256,3072]{1,0:T(8,128)(2,1)S(1)}, bf16[256,3072]{1,0:T(8,128)(2,1)}, u32[]{:S(2)}) copy-start(bf16[256,3072]{1,0:T(8,128)(2,1)} %all-gather.7.cloned.1.call-done) | copy-start | bytes 4718596
  33.8 4.6 %copy-start.12 = (f32[3072]{0:T(1024)S(1)}, f32[3072]{0:T(1024)}, u32[]{:S(2)}) copy-start(f32[3072]{0:T(1024)} %param.16) | copy-start | bytes 36868
  59.9 1.4 copy-start.5
  61.3 3.9 %copy-start.8 = (bf16[256,768]{1,0:T(8,128)(2,1)S(1)}, bf16[256,768]{1,0:T(8,128)(2,1)}, u32[]{:S(2)}) copy-start(bf16[256,768]{1,0:T(8,128)(2,1)} %convolution_convert_fusion.1) | copy-start | bytes 1179652
  65.2 0.9 copy-start.9
  66.1 6.8 %slice-start = ((s8[4718592]{0:T(1024)(128)(4,1)}), s8[524288]{0:T(1024)(128)(4,1)S(1)}, s32[]{:S(2)}) async-start(s8[4718592]{0:T(1024)(128)(4,1)} %bitcast.64), calls=%async_computation.8 | async-start | bytes 1048576
  69.6 3.4 %slice-start.1 = ((s8[4718592]{0:T(1024)(128)(4,1)}), s8[4194304]{0:T(1024)(128)(4,1)S(1)}, s32[]{:S(2)}) async-start(s8[4718592]{0:T(1024)(128)(4,1)} %bitcast.64), calls=%async_computation.9 | async-start | bytes 8388608
  73.1 31.0 %copy-start.6 = (bf16[256,768]{1,0:T(8,128)(2,1)S(1)}, bf16[256,768]{1,0:T(8,128)(2,1)}, u32[]{:S(2)}) copy-start(bf16[256,768]{1,0:T(8,128)(2,1)} %param.15) | copy-start | bytes 1179652
  73.1 38.8 %copy-start.11 = (bf16[768,128]{1,0:T(8,128)(2,1)S(1)}, bf16[768,128]{1,0:T(8,128)(2,1)}, u32[]{:S(2)}) copy-start(bf16[768,128]{1,0:T(8,128)(2,1)} %param.24) | copy-start | bytes 589828
  75.7 69.3 %reduce-scatter.5.cloned.1.call-start = ((), (), s32[]{:S(2)}) async-start(), calls=%async_computation.6 | async-start | bytes 1720320 | tf_op jit(solution)/shard_map/reduce_scatter | solution.py:162
  111.9 33.2 %copy-start.10 = (s32[256]{0:T(256)S(1)}, s32[256]{0:T(256)}, u32[]{:S(2)}) copy-start(s32[256]{0:T(256)} %param.29) | copy-start | bytes 3076
  111.9 124.9 %copy-start.1 = (bf16[320,2048]{1,0:T(8,128)(2,1)S(1)}, bf16[320,2048]{1,0:T(8,128)(2,1)}, u32[]{:S(2)}) copy-start(bf16[320,2048]{1,0:T(8,128)(2,1)} %head_ref.1) | copy-start | bytes 3932164
  111.9 124.9 %copy-start.2 = (bf16[3264,128]{1,0:T(8,128)(2,1)S(1)}, bf16[3264,128]{1,0:T(8,128)(2,1)}, u32[]{:S(2)}) copy-start(bf16[3264,128]{1,0:T(8,128)(2,1)} %tail_ref.1) | copy-start | bytes 2506756
  111.9 124.8 %copy-start.3 = (bf16[640,512]{1,0:T(8,128)(2,1)S(1)}, bf16[640,512]{1,0:T(8,128)(2,1)}, u32[]{:S(2)}) copy-start(bf16[640,512]{1,0:T(8,128)(2,1)} %middle_ref.1) | copy-start | bytes 1966084
  116.8 119.9 %all-gather.9.cloned.1.call-start = ((), (), s32[]{:S(2)}) async-start(), calls=%async_computation.7 | async-start | bytes 11354112 | tf_op jit(solution)/shard_map/all_gather | solution.py:163
  255.7 10.8 %all-to-all-start = ((f32[8,8,256]{2,0,1:T(8,128)}), f32[8,8,256]{2,0,1:T(8,128)S(1)}, u32[]{:S(2)}, u32[]{:S(2)}) async-start(f32[8,8,256]{2,0,1:T(8,128)} %bitcast.9), calls=%async_computation.2 | async-start | bytes 131072 | tf_op jit(solution)/shard_map/all_to_all | solution.py:175
Sparse Core Ops, SparseCore 0:
  9.6 22.3 all-gather.6
  34.1 19.6 all-gather.4
  75.8 28.1 reduce-scatter.2
  116.9 28.0 reduce-scatter.4
  147.8 88.8 all-gather.8

commit v2 on v1

v2 whole, which is shorter than its diff:
```python
import functools

import jax
import jax.numpy as jnp
from jax import lax
from jax.experimental import pallas as pl
from jax.experimental.pallas import tpu as pltpu
from jax.sharding import PartitionSpec as P

HD = 96
NEG_FILL = -1e30
EPS = 1e-06
F32 = jnp.float32
BF16 = jnp.bfloat16


def norm_full(rows, gain):
    wide = rows.astype(F32)
    mean_sq = jnp.mean(wide * wide, axis=1, keepdims=True)
    return (wide * lax.rsqrt(mean_sq + EPS) * gain[None]).astype(BF16)


def project(full_rows, weight):
    return jnp.dot(full_rows, weight, preferred_element_type=F32).astype(BF16)


def chunk_of(rows):
    best = rows
    if rows > 1024:
        for size in range(16, 1025, 16):
            if rows % size == 0:
                best = size
    return best


def band_stats(band, table_ref, goal):
    rows = table_ref.shape[0]
    chunk = chunk_of(rows)
    top = total = pick = None
    for start in range(0, rows, chunk):
        logits = lax.dot_general(
            table_ref[start : start + chunk, :],
            band,
            (((1,), (1,)), ((), ())),
            preferred_element_type=F32,
        )
        word = lax.broadcasted_iota(jnp.int32, logits.shape, 0)
        chosen = jnp.sum(jnp.where(word == goal - start, logits, 0.0), 0, keepdims=True)
        peak = jnp.max(logits, 0, keepdims=True)
        if top is None:
            top = peak
            total = jnp.sum(jnp.exp(logits - top), 0, keepdims=True)
            pick = chosen
        else:
            higher = jnp.maximum(top, peak)
            total = total * jnp.exp(top - higher) + jnp.sum(
                jnp.exp(logits - higher), 0, keepdims=True
            )
            top = higher
            pick = pick + chosen
    return top, total, pick


MESH = pl.DeviceIdType.MESH


def tp_device(rank):
    return {"ctx": lax.axis_index("ctx"), "tp": rank}


def remote(src, dst, send_sem, recv_sem, device):
    return pltpu.make_async_remote_copy(
        src_ref=src,
        dst_ref=dst,
        send_sem=send_sem,
        recv_sem=recv_sem,
        device_id=device,
        device_id_type=MESH,
    )


def reduce_kernel(
    tp_count,
    model_width,
    context_ref,
    w_out_ref,
    hidden_ref,
    gain_ref,
    proj_head_ref,
    proj_middle_ref,
    proj_tail_ref,
    hidden_out_ref,
    own_ref,
    a_send,
    a_recv,
    b_send,
    b_recv,
    part,
    c_recv,
    d_send,
    d_recv,
    sq_part,
    sq_recv,
    a_sems,
    b_sems,
    c_sems,
    d_sems,
    sq_sems,
):
    chips = tp_count // 2
    tp = lax.axis_index("tp")
    chip, core = tp // 2, tp % 2
    partner = tp_device(chip * 2 + 1 - core)
    width = hidden_ref.shape[1]
    rows = own_ref.shape[0]

    barrier = pltpu.get_barrier_semaphore()
    for step in range(1, tp_count):
        pl.semaphore_signal(
            barrier, inc=1, device_id=tp_device((tp + step) % tp_count), device_id_type=MESH
        )
    pl.semaphore_wait(barrier, tp_count - 1)

    def columns(rank):
        return pl.ds(pl.multiple_of(rank * width, width), width)

    def tokens(rank):
        return pl.ds(pl.multiple_of(rank * rows, rows), rows)

    context = context_ref[...]
    order = list(range(1, chips)) + [0]
    pending = []
    acc = None
    for j in order:
        there = (chip + j) % chips
        a_send[j] = jnp.dot(
            context, w_out_ref[:, columns(there * 2 + 1 - core)], preferred_element_type=F32
        ).astype(BF16)
        copy = remote(a_send.at[j], a_recv.at[j], a_sems.at[0, j], a_sems.at[1, j], partner)
        copy.start()
        pending.append(copy)
        mine = jnp.dot(
            context, w_out_ref[:, columns(there * 2 + core)], preferred_element_type=F32
        )
        copy.wait_recv()
        mine = mine + a_recv[j].astype(F32)
        if j > 0:
            b_send[j] = mine.astype(BF16)
            copy = remote(
                b_send.at[j],
                b_recv.at[j],
                b_sems.at[0, j],
                b_sems.at[1, j],
                tp_device(there * 2 + core),
            )
            copy.start()
            pending.append(copy)
        else:
            acc = mine
    for j in range(1, chips):
        remote(b_send.at[j], b_recv.at[j], b_sems.at[0, j], b_sems.at[1, j], partner).wait_recv()
        acc = acc + b_recv[j].astype(F32)
    summed = hidden_ref[...].astype(F32) + acc
    hidden_out_ref[...] = summed.astype(BF16)
    squares = jnp.sum(summed * summed, 1, keepdims=True)
    sq_part[...] = jnp.broadcast_to(squares, sq_part.shape)
    for step in range(1, tp_count):
        there = (tp + step) % tp_count
        copy = remote(
            sq_part.at[tokens(there), :],
            sq_recv.at[step],
            sq_sems.at[0, step],
            sq_sems.at[1, step],
            tp_device(there),
        )
        copy.start()
        pending.append(copy)

    scaled = (summed * gain_ref[...]).astype(BF16)
    first = proj_head_ref.shape[1]
    second = first + proj_middle_ref.shape[1]
    part[:, :first] = jnp.dot(scaled, proj_head_ref[...], preferred_element_type=F32).astype(BF16)
    part[:, first:second] = jnp.dot(
        scaled, proj_middle_ref[...], preferred_element_type=F32
    ).astype(BF16)
    part[:, second:] = jnp.dot(scaled, proj_tail_ref[...], preferred_element_type=F32).astype(BF16)
    for j in order:
        there = (chip + j) % chips
        copy = remote(
            part.at[tokens(there * 2 + 1 - core), :],
            c_recv.at[j],
            c_sems.at[0, j],
            c_sems.at[1, j],
            partner,
        )
        copy.start()
        pending.append(copy)
    acc = None
    for j in order:
        there = (chip + j) % chips
        remote(
            part.at[tokens(there * 2 + 1 - core), :],
            c_recv.at[j],
            c_sems.at[0, j],
            c_sems.at[1, j],
            partner,
        ).wait_recv()
        mine = part[tokens(there * 2 + core), :].astype(F32) + c_recv[j].astype(F32)
        if j > 0:
            d_send[j] = mine.astype(BF16)
            copy = remote(
                d_send.at[j],
                d_recv.at[j],
                d_sems.at[0, j],
                d_sems.at[1, j],
                tp_device(there * 2 + core),
            )
            copy.start()
            pending.append(copy)
        else:
            acc = mine
    total_sq = sq_part[tokens(tp), :]
    for step in range(1, tp_count):
        remote(
            sq_part.at[tokens(tp), :],
            sq_recv.at[step],
            sq_sems.at[0, step],
            sq_sems.at[1, step],
            partner,
        ).wait_recv()
        total_sq = total_sq + sq_recv[step]
    row_scale = lax.rsqrt(total_sq[:, :1] / model_width + EPS)
    for j in range(1, chips):
        remote(d_send.at[j], d_recv.at[j], d_sems.at[0, j], d_sems.at[1, j], partner).wait_recv()
        acc = acc + d_recv[j].astype(F32)
    own_ref[...] = (acc * row_scale).astype(BF16)
    for copy in pending:
        copy.wait_send()


def reduced_bands(context, w_out, hidden_in, gain, proj_head, proj_middle, proj_tail):
    tp_count = lax.axis_size("tp")
    chips = tp_count // 2
    tokens, width = hidden_in.shape
    rows = tokens // tp_count
    bands = proj_head.shape[1] + proj_middle.shape[1] + proj_tail.shape[1]
    return pl.pallas_call(
        functools.partial(reduce_kernel, tp_count, width * tp_count),
        out_shape=(
            jax.ShapeDtypeStruct((tokens, width), BF16),
            jax.ShapeDtypeStruct((rows, bands), BF16),
        ),
        in_specs=[pl.BlockSpec(memory_space=pltpu.VMEM)] * 7,
        out_specs=(pl.BlockSpec(memory_space=pltpu.VMEM),) * 2,
        scratch_shapes=[pltpu.VMEM((chips, tokens, width), BF16)] * 4
        + [pltpu.VMEM((tokens, bands), BF16)]
        + [pltpu.VMEM((chips, rows, bands), BF16)] * 3
        + [pltpu.VMEM((tokens, 128), F32), pltpu.VMEM((tp_count, rows, 128), F32)]
        + [pltpu.SemaphoreType.DMA((2, chips))] * 4
        + [pltpu.SemaphoreType.DMA((2, tp_count))],
        compiler_params=pltpu.CompilerParams(
            collective_id=0, has_side_effects=True, vmem_limit_bytes=48 * 1024 * 1024
        ),
    )(context, w_out, hidden_in, gain, proj_head, proj_middle, proj_tail)


def combined(one, other):
    top = jnp.maximum(one[0], other[0])
    return (
        top,
        one[1] * jnp.exp(one[0] - top) + other[1] * jnp.exp(other[0] - top),
        one[2] + other[2],
    )


def loss_kernel(
    line,
    tp_count,
    own_ref,
    targets_ref,
    clusters_ref,
    head_ref,
    head_pair_ref,
    middle_ref,
    middle_pair_ref,
    tail_ref,
    tail_pair_ref,
    losses_ref,
    bands,
    goals,
    stat_send,
    stat_recv,
    z_send,
    z_recv,
    y_sems,
    c_sems,
    g_sems,
    s_sems,
):
    chips = tp_count // 2
    tp = lax.axis_index("tp")
    ctx = lax.axis_index("ctx")
    chip, core = tp // 2, tp % 2
    spot, side = ctx // 2, ctx % 2
    rows = own_ref.shape[0]
    ctx_count = line * 2
    v0 = head_ref.shape[0] * tp_count * ctx_count
    v1 = middle_ref.shape[0] * tp_count * ctx_count

    def device(place, rank):
        return {"ctx": place * 2 + side, "tp": rank}

    barrier = pltpu.get_barrier_semaphore()
    for k in range(line):
        for t in range(tp_count):
            if k or t:
                pl.semaphore_signal(
                    barrier,
                    inc=1,
                    device_id=device((spot + k) % line, (tp + t) % tp_count),
                    device_id_type=MESH,
                )
    pl.semaphore_wait(barrier, line * tp_count - 1)

    def shard(source, rank):
        return bands.at[source, pl.ds(pl.multiple_of(rank * rows, rows), rows), :]

    def along(d, source, way):
        there = spot + 1 if way == 0 else spot - 1
        piece = shard(source, tp)
        return remote(
            piece, piece, z_send.at[way, d], z_recv.at[way, d + 1], device(there, tp)
        )

    def arrival(d, source, way):
        piece = shard(source, tp)
        return remote(piece, piece, z_send.at[way, d], z_recv.at[way, d], device(spot, tp))

    def sideways(source, j):
        piece = shard(source, tp)
        there = ((chip + j) % chips) * 2 + core
        return remote(
            piece, piece, y_sems.at[0, source, j], y_sems.at[1, source, j], device(spot, there)
        )

    def from_side(source, j):
        piece = shard(source, ((chip - j + chips) % chips) * 2 + core)
        return remote(
            piece, piece, y_sems.at[0, source, j], y_sems.at[1, source, j], device(spot, tp)
        )

    def across(source, j, owner_core):
        piece = shard(source, ((chip - j + chips) % chips) * 2 + owner_core)
        return remote(
            piece,
            piece,
            c_sems.at[0, source, j],
            c_sems.at[1, source, j],
            device(spot, chip * 2 + 1 - core),
        )

    def spread(source):
        for j in range(1, chips):
            sideways(source, j).start()
        across(source, 0, core).start()

    def goal_copy(k):
        return remote(
            goals.at[spot],
            goals.at[spot],
            g_sems.at[0, k],
            g_sems.at[1, k],
            device((spot + k) % line, tp),
        )

    def stat_copy(source, t):
        return remote(
            stat_send.at[source],
            stat_recv.at[spot * tp_count + tp],
            s_sems.at[0, source, t],
            s_sems.at[1, spot, t],
            device(source, (tp + t) % tp_count),
        )

    bands[spot, pl.ds(pl.multiple_of(tp * rows, rows), rows), :] = own_ref[...]
    goals[spot] = targets_ref[...]

    @pl.when(spot + 1 < line)
    def _():
        along(0, spot, 0).start()

    @pl.when(spot > 0)
    def _():
        along(0, spot, 1).start()

    spread(spot)
    for k in range(1, line):
        goal_copy(k).start()
    for k in range(1, line):
        place = (spot - k + line) % line
        remote(
            goals.at[place], goals.at[place], g_sems.at[0, k], g_sems.at[1, k], device(spot, tp)
        ).wait_recv()

    place_own = tp * ctx_count + ctx
    place_pair = tp * ctx_count + spot * 2 + 1 - side
    first = head_ref.shape[1]
    second = first + middle_ref.shape[1]

    def finish(source):
        for j in range(1, chips):
            from_side(source, j).wait_recv()
            across(source, j, core).start()
        for j in range(chips):
            across(source, j, 1 - core).wait_recv()
        goal = goals[source][0:1, :]

        def band(low, high, base, own, pair):
            size = own.shape[0]
            piece = bands[source, :, low:high]
            return combined(
                band_stats(piece, own, goal - base - place_own * size),
                band_stats(piece, pair, goal - base - place_pair * size),
            )

        one = band(0, first, 0, head_ref, head_pair_ref)
        two = band(first, second, v0, middle_ref, middle_pair_ref)
        three = band(second, bands.shape[2], v0 + v1, tail_ref, tail_pair_ref)
        found = (one[0], one[1], two[0], two[1], three[0], three[1], one[2] + two[2] + three[2])
        for i, value in enumerate(found):
            stat_send[source, i : i + 1, :] = value
        stat_send[source, 7:8, :] = jnp.zeros_like(one[0])
        for t in range(1, tp_count):
            stat_copy(source, t).start()

        @pl.when(source != spot)
        def _():
            stat_copy(source, 0).start()

    def step(d, carry):
        @pl.when((d + 1 < line) & (spot - d - 1 >= 0))
        def _():
            source = spot - d - 1
            arrival(d + 1, source, 0).wait_recv()

            @pl.when(spot + 1 < line)
            def _():
                along(d + 1, source, 0).start()

            spread(source)

        @pl.when((d + 1 < line) & (spot + d + 1 < line))
        def _():
            source = spot + d + 1
            arrival(d + 1, source, 1).wait_recv()

            @pl.when(spot > 0)
            def _():
                along(d + 1, source, 1).start()

            spread(source)

        @pl.when(spot - d >= 0)
        def _():
            finish(spot - d)

        @pl.when((d > 0) & (spot + d < line))
        def _():
            finish(spot + d)

        return carry

    lax.fori_loop(0, line, step, 0)

    stat_recv[spot * tp_count + tp] = stat_send[spot]
    clusters = lax.dot_general(
        clusters_ref[...],
        bands[spot, :, :first],
        (((1,), (1,)), ((), ())),
        preferred_element_type=F32,
    )
    for k in range(line):
        place = (spot + k) % line
        for t in range(tp_count):
            if k or t:
                slot = stat_recv.at[place * tp_count + (tp - t + tp_count) % tp_count]
                remote(
                    slot, slot, s_sems.at[0, place, t], s_sems.at[1, place, t], device(spot, tp)
                ).wait_recv()

    def total_of(i):
        tops = stat_recv[:, i, :]
        top = jnp.max(tops, 0, keepdims=True)
        return top + jnp.log(
            jnp.sum(stat_recv[:, i + 1, :] * jnp.exp(tops - top), 0, keepdims=True)
        )

    words = total_of(0)
    middle_total = total_of(2)
    tail_total = total_of(4)
    pick = jnp.sum(stat_recv[:, 6, :], 0, keepdims=True)
    first_cluster, second_cluster = clusters[0:1, :], clusters[1:2, :]
    top = jnp.maximum(words, jnp.maximum(first_cluster, second_cluster))
    head_total = top + jnp.log(
        jnp.exp(words - top) + jnp.exp(first_cluster - top) + jnp.exp(second_cluster - top)
    )
    goal = targets_ref[0:1, :]
    extra = jnp.where(
        goal < v0,
        0.0,
        jnp.where(goal < v0 + v1, middle_total - first_cluster, tail_total - second_cluster),
    )
    losses_ref[...] = head_total + extra - pick

    for k in range(1, line):
        goal_copy(k).wait_send()

    def settle(source, carry):
        for j in range(1, chips):
            sideways(source, j).wait_send()
        for j in range(chips):
            across(source, j, core).wait_send()
        for t in range(1, tp_count):
            stat_copy(source, t).wait_send()

        @pl.when(source != spot)
        def _():
            stat_copy(source, 0).wait_send()

        @pl.when((spot + 1 < line) & (spot - source >= 0))
        def _():
            along(source, spot - source, 0).wait_send()

        @pl.when((spot > 0) & (spot + source < line))
        def _():
            along(source, spot + source, 1).wait_send()

        return carry

    lax.fori_loop(0, line, settle, 0)


def band_losses(own_bands, targets, clusters, tables):
    tp_count = lax.axis_size("tp")
    ctx_count = lax.axis_size("ctx")
    line = ctx_count // 2
    chips = tp_count // 2
    tokens = targets.shape[0]
    width = own_bands.shape[1]
    swap = [(i, i ^ 1) for i in range(ctx_count)]
    paired = []
    for table in tables:
        paired += [table, lax.ppermute(table, "ctx", swap)]
    goals = jnp.broadcast_to(targets[None], (8, tokens))
    clusters = jnp.pad(clusters, ((0, 16 - clusters.shape[0]), (0, 0)))
    dma = pltpu.SemaphoreType.DMA
    return pl.pallas_call(
        functools.partial(loss_kernel, line, tp_count),
        out_shape=jax.ShapeDtypeStruct((1, tokens), F32),
        in_specs=[pl.BlockSpec(memory_space=pltpu.VMEM)] * 9,
        out_specs=pl.BlockSpec(memory_space=pltpu.VMEM),
        scratch_shapes=[
            pltpu.VMEM((line, tokens, width), BF16),
            pltpu.VMEM((line, 8, tokens), jnp.int32),
            pltpu.VMEM((line, 8, tokens), F32),
            pltpu.VMEM((line * tp_count, 8, tokens), F32),
            dma((2, line + 1)),
            dma((2, line + 1)),
            dma((2, line, chips)),
            dma((2, line, chips)),
            dma((2, line)),
            dma((2, line, tp_count)),
        ],
        compiler_params=pltpu.CompilerParams(
            collective_id=1, has_side_effects=True, vmem_limit_bytes=52 * 1024 * 1024
        ),
    )(own_bands, goals, clusters, *paired)[0]


def body(
    hidden_in,
    norm_gain,
    w_query,
    w_key,
    w_value,
    w_out,
    head_gain,
    proj_head,
    proj_middle,
    proj_tail,
    table_head,
    table_middle,
    table_tail,
    clusters,
    targets,
):
    seg_len, local_width = hidden_in.shape
    tp_rank = lax.axis_index("tp")
    ctx_rank = lax.axis_index("ctx")
    ctx_count = lax.axis_size("ctx")

    before = lax.ppermute(hidden_in, "ctx", [(i, i + 1) for i in range(ctx_count - 1)])
    own_full = norm_full(lax.all_gather(hidden_in, "tp", axis=1, tiled=True), norm_gain)
    before_full = norm_full(lax.all_gather(before, "tp", axis=1, tiled=True), norm_gain)

    queries = project(own_full, w_query)
    keys = jnp.concatenate([project(before_full, w_key), project(own_full, w_key)], 0)
    values = jnp.concatenate([project(before_full, w_value), project(own_full, w_value)], 0)
    heads_local = queries.shape[1] // HD
    query_heads = queries.reshape(seg_len, heads_local, HD)
    key_heads = keys.reshape(2 * seg_len, heads_local, HD)
    value_heads = values.reshape(2 * seg_len, heads_local, HD)
    scores = jnp.einsum(
        "qhe,khe->hqk", query_heads, key_heads, preferred_element_type=F32
    ) * HD ** (-0.5)
    row_pos = lax.broadcasted_iota(jnp.int32, (seg_len, 2 * seg_len), 0)
    col_pos = lax.broadcasted_iota(jnp.int32, (seg_len, 2 * seg_len), 1)
    allowed = jnp.where(col_pos < seg_len, ctx_rank > 0, col_pos - seg_len <= row_pos)
    scores = jnp.where(allowed[None], scores, NEG_FILL)
    top_score = jnp.max(scores, axis=2, keepdims=True)
    raised = jnp.exp(scores - top_score)
    weights = (raised / jnp.sum(raised, axis=2, keepdims=True)).astype(BF16)
    context = jnp.einsum("hqk,khe->qhe", weights, value_heads, preferred_element_type=F32)
    context = context.astype(BF16).reshape(seg_len, heads_local * HD)
    gain_out = lax.dynamic_slice_in_dim(head_gain, tp_rank * local_width, local_width)
    hidden_out, own_bands = reduced_bands(
        context, w_out, hidden_in, gain_out[None], proj_head, proj_middle, proj_tail
    )
    losses = band_losses(
        own_bands, targets, clusters, (table_head, table_middle, table_tail)
    )
    return (hidden_out, losses)


def solution(mesh):
    placed = (
        P("ctx", "tp"),
        P(),
        P(None, "tp"),
        P(None, "tp"),
        P(None, "tp"),
        P("tp", None),
        P(),
        P("tp", None),
        P("tp", None),
        P("tp", None),
        P(("tp", "ctx"), None),
        P(("tp", "ctx"), None),
        P(("tp", "ctx"), None),
        P(),
        P("ctx"),
    )
    return jax.shard_map(
        body, mesh=mesh, in_specs=placed, out_specs=(P("ctx", "tp"), P("ctx")), check_vma=False
    )
```

time: 280 us -> 165 us (0.59)
  waiting for transfers between devices: 157 us -> 20.9 us
  Pallas kernels: 18.9 us -> 80.3 us
  blocking collectives: 32.2 us -> 0 us
  matrix products: 36.9 us -> 25.7 us
  local copies, waits for them, and re-layouts: 4.23 us -> 10.8 us
  other arithmetic: 7.23 us -> 3.98 us
    all_gather x1 -> x0, waiting for transfers between devices: 71 us -> none  [body(): bands = lax.all_gather(own_bands, ('ctx', 'tp'), axis=0, tiled=True)]
    pallas_call x1 -> x2, Pallas kernels: 18.9 us -> 80.3 us  [the longest x1 51.4 us: band_losses(): pl.pallas_call(functools.partial(loss_kernel, line, tp_count), out_shape=...]
    reduce_scatter x2 -> x0, waiting for transfers between devices: 55.7 us -> none  [the longest x1 28.2 us: body(): lax.psum_scatter(partial_bands, 'tp', scatter_dimension=0, tiled=True)]
    all_gather x2 -> x0, blocking collectives: 26.3 us -> none  [the longest x1 20.5 us: body(): goals_all = lax.all_gather(targets, 'ctx', axis=0, tiled=True)]
    dot_general x3 -> x0, matrix products: 9.09 us -> none  [the longest x1 4.89 us: body(): jnp.dot(scaled, projection, preferred_element_type=F32).astype(BF16)]
    psum x1 -> x0, blocking collectives: 5.91 us -> none  [body(): square_sums = lax.psum(jnp.sum(summed * summed, 1), 'tp')]
    all_to_all x1 -> x0, waiting for transfers between devices: 5.29 us -> none  [body(): lax.all_to_all(stats.reshape(8, ctx_count, seg_len), 'ctx', split_axis=1,...]
    ppermute x1, waiting for transfers between devices: 8.64 us -> 4.07 us  [body(): lax.ppermute(hidden_in, 'ctx', [(i, i + 1) for i in range(ctx_count - 1)])]
  transfers between devices with their start and end apart: 7 -> 6, of which waited for: 7 -> 3; matrix products, arithmetic and copies ran while one was open for 6% -> 21% of each run, Pallas kernels for 0% -> 18%
where the time goes in v2:
time: 165 us
  Pallas kernels  80.3 us (49%)
  matrix products  25.7 us (16%)
  waiting for transfers between devices  20.9 us (13%)
  between operations  14.3 us (9%)
  local copies, waits for them, and re-layouts  10.8 us (7%)
  starting transfers between devices  8.56 us (5%)
  other arithmetic  3.98 us (2%)
    pallas_call x1, Pallas kernels, band_losses(): pl.pallas_call(functools.partial(loss_kernel, line, tp_count), out_shape=...  51.4 us
    pallas_call x1, Pallas kernels, reduced_bands(): pl.pallas_call(functools.partial(reduce_kernel, tp_count, width * tp_coun...  28.9 us
    dot_general x5, matrix products, project(): return jnp.dot(full_rows, weight, preferred_element_type=F32).astype(BF16)  17.9 us
    all_gather x1, waiting for transfers between devices, body(): lax.all_gather(hidden_in, 'tp', axis=1, tiled=True)  8.44 us
    all_gather x1, waiting for transfers between devices, body(): lax.all_gather(before, 'tp', axis=1, tiled=True)  7.73 us
    unnamed x30, local copies, waits for them, and re-layouts  5.15 us
    ppermute x1, starting transfers between devices, body(): lax.ppermute(hidden_in, 'ctx', [(i, i + 1) for i in range(ctx_count - 1)])  4.87 us
    dot_general x1, matrix products, body(): jnp.einsum('hqk,khe->qhe', weights, value_heads, preferred_element_type=F32)  4.19 us
  transfers between devices with their start and end apart: 6, of which 3 were waited for; matrix products, arithmetic and copies ran while one was open for 21% of the time, Pallas kernels for 18%

profile of v2, /device:TPU:0, one launch (start us, length us, event | category | flops | bytes accessed | tf_op | source)
XLA Modules:
  0.0 164.7 jit_solution(7109038378292039360)
XLA Ops:
  7.2 0.0 all-gather.5.cloned.1.call-start
  7.2 0.7 all-gather.5.cloned.1.call-update
  7.9 0.0 all-gather.3.cloned.1.call-start
  7.9 4.9 %collective-permute-start = (bf16[256,768]{1,0:T(8,128)(2,1)}, bf16[256,768]{1,0:T(8,128)(2,1)S(1)}, u32[]{:S(2)}, u32[]{:S(2)}) collective-permute-start(bf16[256,768]{1,0:T(8,128)(2,1)} %hidden_ref.1), channel_id=1, source_target_pairs={{0,4},{4,8},{8,12},{12,16},{16,20},{20,24},{24,28},{1,5},{5,9},{9,... | collective-permute-start | bytes 1179656 | tf_op jit(solution)/shard_map/ppermute | solution.py:602
  12.8 1.6 collective-permute-start.1
  14.4 0.5 collective-permute-start.2
  14.9 1.5 collective-permute-start.3
  16.4 0.8 dynamic_slice.3
  17.2 1.3 pad.4.clusters_ref
  18.5 4.1 %collective-permute-done = bf16[256,768]{1,0:T(8,128)(2,1)S(1)} collective-permute-done((bf16[256,768]{1,0:T(8,128)(2,1)}, bf16[256,768]{1,0:T(8,128)(2,1)S(1)}, u32[]{:S(2)}, u32[]{:S(2)}) %collective-permute-start) | collective-permute-done | bytes 393248 | tf_op jit(solution)/shard_map/ppermute | solution.py:602
  22.6 0.7 copy-done.9
  23.4 0.0 all-gather.3.cloned.1.call-update
  23.4 0.1 fusion.13
  23.5 8.4 %all-gather.5.cloned.1.call-done = bf16[256,3072]{1,0:T(8,128)(2,1)} async-done(((bf16[256,768]{1,0:T(8,128)(2,1)}), bf16[256,3072]{1,0:T(8,128)(2,1)}) %all-gather.5.cloned.1.call-update) | async-done | bytes 1572880 | tf_op jit(solution)/shard_map/all_gather | solution.py:603
  32.0 1.8 %fusion.5 = f32[256]{0:T(256)S(1)} fusion(bf16[256,3072]{1,0:T(8,128)(2,1)} %all-gather.5.cloned.1.call-done), kind=kLoop, calls=%fused_computation.12 | loop fusion | flops 2359040 | bytes 1573888 | tf_op jit(solution)/shard_map/reduce_sum | solution.py:19
  33.8 0.0 copy-start.11
  33.8 4.4 %convolution_convert_fusion.2 = bf16[256,768]{1,0:T(8,128)(2,1)S(1)} fusion(bf16[3072,768]{1,0:T(8,128)(2,1)} %param.17, bf16[256,3072]{1,0:T(8,128)(2,1)} %all-gather.5.cloned.1.call-done, f32[256]{0:T(256)S(1)} %add_rsqrt_fusion, f32[3072]{0:T(1024)} %param.16), kind=kOutput, calls=%fused_computation.22 | convolution fusion | flops 1211301888 | bytes 6697984 | tf_op jit(solution)/shard_map/dot_general | solution.py:24
  38.2 0.2 copy.22
  38.3 0.0 copy-done.7
  38.4 0.0 copy-done.11
  38.4 3.9 %convolution_convert_fusion.3 = bf16[256,768]{1,0:T(8,128)(2,1)S(1)} fusion(bf16[3072,768]{1,0:T(8,128)(2,1)} %param.19, bf16[256,3072]{1,0:T(8,128)(2,1)S(1)} %copy-done.7, f32[256]{0:T(256)S(1)} %add_rsqrt_fusion, f32[3072]{0:T(1024)S(1)} %copy-done.11), kind=kOutput, calls=%fused_computation.23 | convolution fusion | flops 1211301888 | bytes 6697984 | tf_op jit(solution)/shard_map/dot_general | solution.py:24
  42.3 3.8 %convolution_convert_fusion = bf16[256,768]{1,0:T(8,128)(2,1)S(1)} fusion(bf16[3072,768]{1,0:T(8,128)(2,1)} %param.18, bf16[256,3072]{1,0:T(8,128)(2,1)S(1)} %copy-done.7, f32[256]{0:T(256)S(1)} %add_rsqrt_fusion, f32[3072]{0:T(1024)S(1)} %copy-done.11), kind=kOutput, calls=%fused_computation.20 | convolution fusion | flops 1211301888 | bytes 6697984 | tf_op jit(solution)/shard_map/dot_general | solution.py:24
  46.1 7.7 %all-gather.3.cloned.1.call-done = bf16[256,3072]{1,0:T(8,128)(2,1)} async-done(((bf16[256,768]{1,0:T(8,128)(2,1)}), bf16[256,3072]{1,0:T(8,128)(2,1)}) %all-gather.3.cloned.1.call-update) | async-done | bytes 1572880 | tf_op jit(solution)/shard_map/all_gather | solution.py:604
  53.8 1.9 %fusion.2 = f32[256]{0:T(256)S(1)} fusion(bf16[256,3072]{1,0:T(8,128)(2,1)} %all-gather.3.cloned.1.call-done), kind=kLoop, calls=%fused_computation.9 | loop fusion | flops 2359040 | bytes 1573888 | tf_op jit(solution)/shard_map/reduce_sum | solution.py:19
  55.8 0.0 slice-start.1
  55.8 4.4 %convolution_convert_fusion.4 = bf16[256,768]{1,0:T(8,128)(2,1)S(1)} fusion(bf16[3072,768]{1,0:T(8,128)(2,1)} %param.19, bf16[256,3072]{1,0:T(8,128)(2,1)} %all-gather.3.cloned.1.call-done, f32[3072]{0:T(1024)S(1)} %copy-done.11, f32[256]{0:T(256)S(1)} %add_rsqrt_fusion.1), kind=kOutput, calls=%fused_computation.24 | convolution fusion | flops 1211301888 | bytes 6697984 | tf_op jit(solution)/shard_map/dot_general | solution.py:24
  60.2 0.0 slice-done
  60.2 0.0 copy-done.8
  60.2 0.0 slice-done.1
  60.2 1.5 convolution_convert_fusion.1
  61.7 0.1 pad_maximum_fusion.1
  61.8 0.3 copy.23
  62.0 3.6 %fusion.23 = (f32[8,256]{1,0:T(8,128)S(1)}, f32[8,256,512]{2,1,0:T(8,128)}) fusion(pred[256,512]{1,0:T(8,128)(4,1)S(1)} %fusion.13, bf16[256,8,96]{0,2,1:T(8,128)(2,1)S(1)} %bitcast.20, bf16[512,8,96]{0,2,1:T(8,128)(2,1)S(1)} %bitcast.18), kind=kOutput, calls=%fused_computation.36 | convolution fusion | flops 205521408 | bytes 5513216 | tf_op jit(solution)/shard_map/sub | solution.py:621
  65.7 0.1 pad_maximum_fusion
  65.7 1.2 copy.21
  66.9 4.2 %fusion.12 = bf16[8,96,256]{2,1,0:T(8,128)(2,1)} fusion(bf16[512,8,96]{0,2,1:T(8,128)(2,1)} %bitcast.19, f32[8,256,512]{2,1,0:T(8,128)} %get-tuple-element.7, f32[8,256]{1,0:T(8,128)S(1)} %get-tuple-element.6), kind=kOutput, calls=%fused_computation.19 | convolution fusion | flops 203620352 | bytes 5382144 | tf_op jit(solution)/shard_map/hqk,khe->qhe/dot_general | solution.py:623
  71.1 1.9 %copy.24.context_ref = bf16[256,768]{1,0:T(8,128)(2,1)} copy(bf16[256,768]{0,1:T(8,128)(2,1)} %bitcast.21) | data formatting | bytes 786432 | tf_op jit(solution)/shard_map/reshape | solution.py:624
  73.1 0.0 copy-done.1
  73.1 1.0 copy-done.2
  74.1 1.1 copy-done.3
  75.2 0.9 copy-done.6
  76.1 28.9 %shard_map.158 = (bf16[256,768]{1,0:T(8,128)(2,1)S(1)}, bf16[64,2688]{1,0:T(8,128)(2,1)S(1)}) custom-call(bf16[256,768]{1,0:T(8,128)(2,1)S(1)} %copy-done.2, bf16[768,3072]{1,0:T(8,128)(2,1)} %w_out_ref.1, bf16[256,768]{1,0:T(8,128)(2,1)S(1)} %copy-done.1, f32[1,768]{1,0:T(1,128)S(1)} %broadcast_in_dim.35.gain_ref, bf16[768,2048]{1,0:T(8,128)(2,1)S(1)} %copy-done, ...), custom_call_target="tpu_custom_call" | custom-call | tf_op jit(solution)/shard_map/pallas_call | solution.py:247
  105.1 0.0 collective-permute-done.2.middle_pair_ref
  105.1 0.0 collective-permute-done.3.tail_pair_ref
  105.1 0.0 collective-permute-done.1.head_pair_ref
  105.1 51.4 %shard_map.159 = f32[1,256]{1,0:T(1,128)S(1)} custom-call(bf16[64,2688]{1,0:T(8,128)(2,1)S(1)} %get-tuple-element.5.own_ref, s32[8,256]{1,0:T(8,128)S(1)} %broadcast_in_dim.36.targets_ref, bf16[16,2048]{1,0:T(8,128)(2,1)S(1)} %copy-done.5, bf16[320,2048]{1,0:T(8,128)(2,1)} %head_ref.1, bf16[320,2048]{1,0:T(8,128)(2,1)} %collective-permute-done.1.head_pair_ref, ...), custom_call_target="tpu_custom_call" | custom-call | tf_op jit(solution)/shard_map/pallas_call | solution.py:557
  156.5 0.7 copy.27
  157.3 0.6 copy.28
  (23 shorter events, 0.1 us)
Async XLA Ops:
  7.2 24.8 %all-gather.5.cloned.1.call-start = ((), (), s32[]{:S(2)}) async-start(), calls=%async_computation.1 | async-start | bytes 1966080 | tf_op jit(solution)/shard_map/all_gather | solution.py:603
  7.9 45.9 %all-gather.3.cloned.1.call-start = ((), (), s32[]{:S(2)}) async-start(), calls=%async_computation | async-start | bytes 1966080 | tf_op jit(solution)/shard_map/all_gather | solution.py:604
  7.9 14.7 %collective-permute-start = (bf16[256,768]{1,0:T(8,128)(2,1)}, bf16[256,768]{1,0:T(8,128)(2,1)S(1)}, u32[]{:S(2)}, u32[]{:S(2)}) collective-permute-start(bf16[256,768]{1,0:T(8,128)(2,1)} %hidden_ref.1), channel_id=1, source_target_pairs={{0,4},{4,8},{8,12},{12,16},{16,20},{20,24},{24,28},{1,5},{5,9},{9,... | collective-permute-start | bytes 1179656 | tf_op jit(solution)/shard_map/ppermute | solution.py:602
  12.8 92.3 %collective-permute-start.1 = (bf16[320,2048]{1,0:T(8,128)(2,1)}, bf16[320,2048]{1,0:T(8,128)(2,1)}, u32[]{:S(2)}, u32[]{:S(2)}) collective-permute-start(bf16[320,2048]{1,0:T(8,128)(2,1)} %head_ref.1), channel_id=1, source_target_pairs={{0,4},{4,0},{8,12},{12,8},{16,20},{20,16},{24,28},{28,24},{1,5},{5... | collective-permute-start | bytes 3932168 | tf_op jit(solution)/shard_map/ppermute | solution.py:553
  14.4 90.7 %collective-permute-start.2 = (bf16[640,512]{1,0:T(8,128)(2,1)}, bf16[640,512]{1,0:T(8,128)(2,1)}, u32[]{:S(2)}, u32[]{:S(2)}) collective-permute-start(bf16[640,512]{1,0:T(8,128)(2,1)} %middle_ref.1), channel_id=1, source_target_pairs={{0,4},{4,0},{8,12},{12,8},{16,20},{20,16},{24,28},{28,24},{1,5},{5... | collective-permute-start | bytes 1966088 | tf_op jit(solution)/shard_map/ppermute | solution.py:553
  14.9 90.2 %collective-permute-start.3 = (bf16[3264,128]{1,0:T(8,128)(2,1)}, bf16[3264,128]{1,0:T(8,128)(2,1)}, u32[]{:S(2)}, u32[]{:S(2)}) collective-permute-start(bf16[3264,128]{1,0:T(8,128)(2,1)} %tail_ref.1), channel_id=1, source_target_pairs={{0,4},{4,0},{8,12},{12,8},{16,20},{20,16},{24,28},{28,24},{1,5},{5... | collective-permute-start | bytes 2506760 | tf_op jit(solution)/shard_map/ppermute | solution.py:553
  22.6 0.7 copy-start.9
  33.8 4.6 %copy-start.7 = (bf16[256,3072]{1,0:T(8,128)(2,1)S(1)}, bf16[256,3072]{1,0:T(8,128)(2,1)}, u32[]{:S(2)}) copy-start(bf16[256,3072]{1,0:T(8,128)(2,1)} %all-gather.5.cloned.1.call-done) | copy-start | bytes 4718596
  33.8 4.6 %copy-start.11 = (f32[3072]{0:T(1024)S(1)}, f32[3072]{0:T(1024)}, u32[]{:S(2)}) copy-start(f32[3072]{0:T(1024)} %param.16) | copy-start | bytes 36868
  53.8 6.4 %slice-start = ((s8[4718592]{0:T(1024)(128)(4,1)}), s8[4194304]{0:T(1024)(128)(4,1)S(1)}, s32[]{:S(2)}) async-start(s8[4718592]{0:T(1024)(128)(4,1)} %bitcast.22), calls=%async_computation.2 | async-start | bytes 8388608
  55.8 4.4 %copy-start.8 = (bf16[256,3072]{1,0:T(8,128)(2,1)S(1)}, bf16[256,3072]{1,0:T(8,128)(2,1)}, u32[]{:S(2)}) copy-start(bf16[256,3072]{1,0:T(8,128)(2,1)} %all-gather.3.cloned.1.call-done) | copy-start | bytes 4718596
  55.8 4.4 %slice-start.1 = ((s8[4718592]{0:T(1024)(128)(4,1)}), s8[524288]{0:T(1024)(128)(4,1)S(1)}, s32[]{:S(2)}) async-start(s8[4718592]{0:T(1024)(128)(4,1)} %bitcast.22), calls=%async_computation.3 | async-start | bytes 1048576
  66.9 6.1 %copy-start = (bf16[768,2048]{1,0:T(8,128)(2,1)S(1)}, bf16[768,2048]{1,0:T(8,128)(2,1)}, u32[]{:S(2)}) copy-start(bf16[768,2048]{1,0:T(8,128)(2,1)} %proj_head_ref.1) | copy-start | bytes 9437188
  66.9 6.1 %copy-start.1 = (bf16[256,768]{1,0:T(8,128)(2,1)S(1)}, bf16[256,768]{1,0:T(8,128)(2,1)}, u32[]{:S(2)}) copy-start(bf16[256,768]{1,0:T(8,128)(2,1)} %hidden_ref.1) | copy-start | bytes 1179652
  73.1 1.0 copy-start.2
  74.1 1.1 copy-start.3
  75.2 0.9 copy-start.6
  76.1 29.0 %copy-start.10 = (s32[256]{0:T(256)S(1)}, s32[256]{0:T(256)}, u32[]{:S(2)}) copy-start(s32[256]{0:T(256)} %param.29) | copy-start | bytes 3076
  76.1 29.0 %copy-start.4 = (bf16[640,512]{1,0:T(8,128)(2,1)S(1)}, bf16[640,512]{1,0:T(8,128)(2,1)}, u32[]{:S(2)}) copy-start(bf16[640,512]{1,0:T(8,128)(2,1)} %middle_ref.1) | copy-start | bytes 1966084
  76.1 29.0 %copy-start.5 = (bf16[16,2048]{1,0:T(8,128)(2,1)S(1)}, bf16[16,2048]{1,0:T(8,128)(2,1)}, u32[]{:S(2)}) copy-start(bf16[16,2048]{1,0:T(8,128)(2,1)} %pad.4.clusters_ref) | copy-start | bytes 196612
Sparse Core Ops, SparseCore 0:
  9.6 22.3 all-gather.4
  34.1 19.6 all-gather.2

commit v3 on v2

--- a/solution.py
+++ b/solution.py
@@ -12,16 +12,6 @@
 EPS = 1e-06
 F32 = jnp.float32
 BF16 = jnp.bfloat16
-
-
-def norm_full(rows, gain):
-    wide = rows.astype(F32)
-    mean_sq = jnp.mean(wide * wide, axis=1, keepdims=True)
-    return (wide * lax.rsqrt(mean_sq + EPS) * gain[None]).astype(BF16)
-
-
-def project(full_rows, weight):
-    return jnp.dot(full_rows, weight, preferred_element_type=F32).astype(BF16)
 
 
 def chunk_of(rows):
@@ -79,34 +69,23 @@
     )
 
 
-def reduce_kernel(
+def reduce_phase(
     tp_count,
     model_width,
     context_ref,
     w_out_ref,
     hidden_ref,
     gain_ref,
-    proj_head_ref,
-    proj_middle_ref,
-    proj_tail_ref,
+    proj_refs,
     hidden_out_ref,
     own_ref,
-    a_send,
-    a_recv,
-    b_send,
-    b_recv,
-    part,
-    c_recv,
-    d_send,
-    d_recv,
-    sq_part,
-    sq_recv,
-    a_sems,
-    b_sems,
-    c_sems,
-    d_sems,
-    sq_sems,
+    buffers,
+    sems,
+    loads,
 ):
+    a_send, a_recv, b_send, b_recv, part, c_recv, d_send, d_recv, sq_part, sq_recv = buffers
+    a_sems, b_sems, c_sems, d_sems, sq_sems = sems
+    proj_head_ref, proj_middle_ref, proj_tail_ref = proj_refs
     chips = tp_count // 2
     tp = lax.axis_index("tp")
     chip, core = tp // 2, tp % 2
@@ -114,19 +93,13 @@
     width = hidden_ref.shape[1]
     rows = own_ref.shape[0]
 
-    barrier = pltpu.get_barrier_semaphore()
-    for step in range(1, tp_count):
-        pl.semaphore_signal(
-            barrier, inc=1, device_id=tp_device((tp + step) % tp_count), device_id_type=MESH
-        )
-    pl.semaphore_wait(barrier, tp_count - 1)
-
     def columns(rank):
         return pl.ds(pl.multiple_of(rank * width, width), width)
 
     def tokens(rank):
         return pl.ds(pl.multiple_of(rank * rows, rows), rows)
 
+    loads[0].wait()
     context = context_ref[...]
     order = list(range(1, chips)) + [0]
     pending = []
@@ -176,7 +149,9 @@
         copy.start()
         pending.append(copy)
 
-    scaled = (summed * gain_ref[...]).astype(BF16)
+    scaled = (summed * gain_ref[:, columns(tp)]).astype(BF16)
+    for load in loads[1:]:
+        load.wait()
     first = proj_head_ref.shape[1]
     second = first + proj_middle_ref.shape[1]
     part[:, :first] = jnp.dot(scaled, proj_head_ref[...], preferred_element_type=F32).astype(BF16)
@@ -238,32 +213,6 @@
         copy.wait_send()
 
 
-def reduced_bands(context, w_out, hidden_in, gain, proj_head, proj_middle, proj_tail):
-    tp_count = lax.axis_size("tp")
-    chips = tp_count // 2
-    tokens, width = hidden_in.shape
-    rows = tokens // tp_count
-    bands = proj_head.shape[1] + proj_middle.shape[1] + proj_tail.shape[1]
-    return pl.pallas_call(
-        functools.partial(reduce_kernel, tp_count, width * tp_count),
-        out_shape=(
-            jax.ShapeDtypeStruct((tokens, width), BF16),
-            jax.ShapeDtypeStruct((rows, bands), BF16),
-        ),
-        in_specs=[pl.BlockSpec(memory_space=pltpu.VMEM)] * 7,
-        out_specs=(pl.BlockSpec(memory_space=pltpu.VMEM),) * 2,
-        scratch_shapes=[pltpu.VMEM((chips, tokens, width), BF16)] * 4
-        + [pltpu.VMEM((tokens, bands), BF16)]
-        + [pltpu.VMEM((chips, rows, bands), BF16)] * 3
-        + [pltpu.VMEM((tokens, 128), F32), pltpu.VMEM((tp_count, rows, 128), F32)]
-        + [pltpu.SemaphoreType.DMA((2, chips))] * 4
-        + [pltpu.SemaphoreType.DMA((2, tp_count))],
-        compiler_params=pltpu.CompilerParams(
-            collective_id=0, has_side_effects=True, vmem_limit_bytes=48 * 1024 * 1024
-        ),
-    )(context, w_out, hidden_in, gain, proj_head, proj_middle, proj_tail)
-
-
 def combined(one, other):
     top = jnp.maximum(one[0], other[0])
     return (
@@ -273,30 +222,22 @@
     )
 
 
-def loss_kernel(
+def loss_phase(
     line,
     tp_count,
     own_ref,
     targets_ref,
     clusters_ref,
-    head_ref,
-    head_pair_ref,
-    middle_ref,
-    middle_pair_ref,
-    tail_ref,
-    tail_pair_ref,
+    table_refs,
     losses_ref,
-    bands,
-    goals,
-    stat_send,
-    stat_recv,
-    z_send,
-    z_recv,
-    y_sems,
-    c_sems,
-    g_sems,
-    s_sems,
+    buffers,
+    sems,
+    loads,
+    swaps,
 ):
+    head_ref, head_pair_ref, middle_ref, middle_pair_ref, tail_ref, tail_pair_ref = table_refs
+    bands, goals, stat_send, stat_recv = buffers
+    z_send, z_recv, y_sems, c_sems, g_sems, s_sems = sems
     chips = tp_count // 2
     tp = lax.axis_index("tp")
     ctx = lax.axis_index("ctx")
@@ -310,18 +251,6 @@
     def device(place, rank):
         return {"ctx": place * 2 + side, "tp": rank}
 
-    barrier = pltpu.get_barrier_semaphore()
-    for k in range(line):
-        for t in range(tp_count):
-            if k or t:
-                pl.semaphore_signal(
-                    barrier,
-                    inc=1,
-                    device_id=device((spot + k) % line, (tp + t) % tp_count),
-                    device_id_type=MESH,
-                )
-    pl.semaphore_wait(barrier, line * tp_count - 1)
-
     def shard(source, rank):
         return bands.at[source, pl.ds(pl.multiple_of(rank * rows, rows), rows), :]
 
@@ -402,6 +331,10 @@
             goals.at[place], goals.at[place], g_sems.at[0, k], g_sems.at[1, k], device(spot, tp)
         ).wait_recv()
 
+    for load in loads:
+        load.wait()
+    for swap in swaps:
+        swap.wait()
     place_own = tp * ctx_count + ctx
     place_pair = tp * ctx_count + spot * 2 + 1 - side
     first = head_ref.shape[1]
@@ -540,41 +473,245 @@
     lax.fori_loop(0, line, settle, 0)
 
 
-def band_losses(own_bands, targets, clusters, tables):
-    tp_count = lax.axis_size("tp")
-    ctx_count = lax.axis_size("ctx")
-    line = ctx_count // 2
+def attention_phase(
+    tp_count,
+    ctx_count,
+    hidden_ref,
+    gain_ref,
+    weights,
+    loads,
+    swaps,
+    buffers,
+    sems,
+):
+    rows, normed, queries, keys, values, acc, context_ref = buffers
+    p_sems, y_sems, c_sems = sems
     chips = tp_count // 2
-    tokens = targets.shape[0]
-    width = own_bands.shape[1]
-    swap = [(i, i ^ 1) for i in range(ctx_count)]
-    paired = []
-    for table in tables:
-        paired += [table, lax.ppermute(table, "ctx", swap)]
-    goals = jnp.broadcast_to(targets[None], (8, tokens))
-    clusters = jnp.pad(clusters, ((0, 16 - clusters.shape[0]), (0, 0)))
-    dma = pltpu.SemaphoreType.DMA
-    return pl.pallas_call(
-        functools.partial(loss_kernel, line, tp_count),
-        out_shape=jax.ShapeDtypeStruct((1, tokens), F32),
-        in_specs=[pl.BlockSpec(memory_space=pltpu.VMEM)] * 9,
-        out_specs=pl.BlockSpec(memory_space=pltpu.VMEM),
-        scratch_shapes=[
-            pltpu.VMEM((line, tokens, width), BF16),
-            pltpu.VMEM((line, 8, tokens), jnp.int32),
-            pltpu.VMEM((line, 8, tokens), F32),
-            pltpu.VMEM((line * tp_count, 8, tokens), F32),
-            dma((2, line + 1)),
-            dma((2, line + 1)),
-            dma((2, line, chips)),
-            dma((2, line, chips)),
-            dma((2, line)),
-            dma((2, line, tp_count)),
-        ],
-        compiler_params=pltpu.CompilerParams(
-            collective_id=1, has_side_effects=True, vmem_limit_bytes=52 * 1024 * 1024
-        ),
-    )(own_bands, goals, clusters, *paired)[0]
+    tp = lax.axis_index("tp")
+    ctx = lax.axis_index("ctx")
+    chip, core = tp // 2, tp % 2
+    seg_len, width = hidden_ref.shape
+    group = 4 * HD
+
+    def shard(part, rank):
+        return rows.at[part, :, pl.ds(pl.multiple_of(rank * width, width), width)]
+
+    def sideways(part, j):
+        piece = shard(part, tp)
+        there = ((chip + j) % chips) * 2 + core
+        return remote(
+            piece, piece, y_sems.at[0, part, j], y_sems.at[1, part, j], tp_device(there)
+        )
+
+    def from_side(part, j):
+        piece = shard(part, ((chip - j + chips) % chips) * 2 + core)
+        return remote(piece, piece, y_sems.at[0, part, j], y_sems.at[1, part, j], tp_device(tp))
+
+    def across(part, j, owner_core):
+        piece = shard(part, ((chip - j + chips) % chips) * 2 + owner_core)
+        return remote(
+            piece,
+            piece,
+            c_sems.at[0, part, j],
+            c_sems.at[1, part, j],
+            tp_device(chip * 2 + 1 - core),
+        )
+
+    def spread(part):
+        for j in range(1, chips):
+            sideways(part, j).start()
+        across(part, 0, core).start()
+
+    def relay(part):
+        for j in range(1, chips):
+            from_side(part, j).wait_recv()
+            across(part, j, core).start()
+
+    def normalise(part):
+        for j in range(chips):
+            across(part, j, 1 - core).wait_recv()
+        wide = rows[part].astype(F32)
+        mean_sq = jnp.mean(wide * wide, axis=1, keepdims=True)
+        normed[...] = (wide * lax.rsqrt(mean_sq + EPS) * gain_ref[...]).astype(BF16)
+
+    def project(weight, out, start):
+        def tile(i, carry):
+            cut = pl.ds(pl.multiple_of(i * group, group), group)
+            out[start : start + seg_len, cut] = jnp.dot(
+                normed[...], weight[:, cut], preferred_element_type=F32
+            ).astype(BF16)
+            return carry
+
+        lax.fori_loop(0, width // group, tile, 0)
+
+    rows[1, :, pl.ds(pl.multiple_of(tp * width, width), width)] = hidden_ref[...]
+    forward = remote(
+        shard(1, tp),
+        shard(0, tp),
+        p_sems.at[0],
+        p_sems.at[1],
+        {"ctx": (ctx + 1) % ctx_count, "tp": tp},
+    )
+    forward.start()
+    spread(1)
+    relay(1)
+    forward.wait_recv()
+    spread(0)
+    for swap in swaps:
+        swap.start()
+    normalise(1)
+    for load in loads:
+        load.wait()
+    project(weights[0], queries, 0)
+    project(weights[1], keys, seg_len)
+    project(weights[2], values, seg_len)
+    relay(0)
+    normalise(0)
+    project(weights[1], keys, 0)
+    project(weights[2], values, 0)
+
+    def heads(i, carry):
+        for h in range(4):
+            low = h * HD // 128 * 128
+            high = -(-(h + 1) * HD // 128) * 128
+            cut = pl.ds(pl.multiple_of(i * group + low, 128), high - low)
+            lane = lax.broadcasted_iota(jnp.int32, (seg_len, high - low), 1) + low
+            inside = (lane >= h * HD) & (lane < (h + 1) * HD)
+            query = jnp.where(inside, queries[:, cut].astype(F32), 0.0).astype(BF16)
+            scores = lax.dot_general(
+                query, keys[:, cut], (((1,), (1,)), ((), ())), preferred_element_type=F32
+            ) * HD ** (-0.5)
+            row_pos = lax.broadcasted_iota(jnp.int32, scores.shape, 0)
+            col_pos = lax.broadcasted_iota(jnp.int32, scores.shape, 1)
+            first = jnp.where(ctx > 0, 0, seg_len)
+            allowed = (col_pos >= first) & (col_pos - seg_len <= row_pos)
+            scores = jnp.where(allowed, scores, NEG_FILL)
+            raised = jnp.exp(scores - jnp.max(scores, axis=1, keepdims=True))
+            shares = (raised / jnp.sum(raised, axis=1, keepdims=True)).astype(BF16)
+            mixed = jnp.dot(shares, values[:, cut], preferred_element_type=F32)
+            acc[:, cut] = jnp.where(inside, mixed, acc[:, cut])
+        return carry
+
+    acc[...] = jnp.zeros_like(acc)
+    lax.fori_loop(0, width // group, heads, 0)
+    context_ref[...] = acc[...].astype(BF16)
+
+    forward.wait_send()
+    for part in range(2):
+        for j in range(1, chips):
+            sideways(part, j).wait_send()
+        for j in range(chips):
+            across(part, j, core).wait_send()
+
+
+def layer_kernel(line, tp_count, *refs):
+    (
+        hidden_ref,
+        norm_gain_ref,
+        head_gain_ref,
+        clusters_ref,
+        targets_ref,
+        wq_ref,
+        wk_ref,
+        wv_ref,
+        wo_ref,
+        ph_ref,
+        pm_ref,
+        pt_ref,
+        th_ref,
+        tm_ref,
+        tt_ref,
+        hidden_out_ref,
+        losses_ref,
+    ) = refs[:17]
+    held = refs[17:30]
+    weights, proj = held[0:4], held[4:7]
+    tables = held[7:13]
+    attention = refs[30:37]
+    own = refs[37]
+    reduce = refs[38:48]
+    loss = refs[48:52]
+    load_sems, swap_sems = refs[52:54]
+    attention_sems = refs[54:57]
+    reduce_sems = refs[57:62]
+    loss_sems = refs[62:68]
+    ctx_count = line * 2
+    tp = lax.axis_index("tp")
+    ctx = lax.axis_index("ctx")
+    spot, side = ctx // 2, ctx % 2
+
+    sources = (wq_ref, wk_ref, wv_ref, wo_ref, ph_ref, pm_ref, pt_ref, th_ref, tm_ref, tt_ref)
+    targets = weights + proj + tables[0::2]
+    loads = [
+        pltpu.make_async_copy(source, target, load_sems.at[i])
+        for i, (source, target) in enumerate(zip(sources, targets))
+    ]
+    for load in loads:
+        load.start()
+
+    barrier = pltpu.get_barrier_semaphore()
+    peers = [
+        {"ctx": ((spot + k) % line) * 2 + side, "tp": (tp + t) % tp_count}
+        for k in range(line)
+        for t in range(tp_count)
+        if k or t
+    ]
+    peers += [
+        {"ctx": (ctx + 1) % ctx_count, "tp": tp},
+        {"ctx": (ctx + ctx_count - 1) % ctx_count, "tp": tp},
+    ]
+    for peer in peers:
+        pl.semaphore_signal(barrier, inc=1, device_id=peer, device_id_type=MESH)
+    pl.semaphore_wait(barrier, len(peers))
+
+    swaps = [
+        remote(
+            source,
+            tables[2 * i + 1],
+            swap_sems.at[0, i],
+            swap_sems.at[1, i],
+            {"ctx": spot * 2 + 1 - side, "tp": tp},
+        )
+        for i, source in enumerate((th_ref, tm_ref, tt_ref))
+    ]
+    attention_phase(
+        tp_count,
+        ctx_count,
+        hidden_ref,
+        norm_gain_ref,
+        weights,
+        loads[:3],
+        swaps,
+        attention,
+        attention_sems,
+    )
+    reduce_phase(
+        tp_count,
+        norm_gain_ref.shape[1],
+        attention[-1],
+        weights[3],
+        hidden_ref,
+        head_gain_ref,
+        proj,
+        hidden_out_ref,
+        own,
+        reduce,
+        reduce_sems,
+        loads[3:7],
+    )
+    loss_phase(
+        line,
+        tp_count,
+        own,
+        targets_ref,
+        clusters_ref,
+        tables,
+        losses_ref,
+        loss,
+        loss_sems,
+        loads[7:],
+        swaps,
+    )
 
 
 def body(
@@ -594,42 +731,73 @@
     clusters,
     targets,
 ):
-    seg_len, local_width = hidden_in.shape
-    tp_rank = lax.axis_index("tp")
-    ctx_rank = lax.axis_index("ctx")
-    ctx_count = lax.axis_size("ctx")
-
-    before = lax.ppermute(hidden_in, "ctx", [(i, i + 1) for i in range(ctx_count - 1)])
-    own_full = norm_full(lax.all_gather(hidden_in, "tp", axis=1, tiled=True), norm_gain)
-    before_full = norm_full(lax.all_gather(before, "tp", axis=1, tiled=True), norm_gain)
-
-    queries = project(own_full, w_query)
-    keys = jnp.concatenate([project(before_full, w_key), project(own_full, w_key)], 0)
-    values = jnp.concatenate([project(before_full, w_value), project(own_full, w_value)], 0)
-    heads_local = queries.shape[1] // HD
-    query_heads = queries.reshape(seg_len, heads_local, HD)
-    key_heads = keys.reshape(2 * seg_len, heads_local, HD)
-    value_heads = values.reshape(2 * seg_len, heads_local, HD)
-    scores = jnp.einsum(
-        "qhe,khe->hqk", query_heads, key_heads, preferred_element_type=F32
-    ) * HD ** (-0.5)
-    row_pos = lax.broadcasted_iota(jnp.int32, (seg_len, 2 * seg_len), 0)
-    col_pos = lax.broadcasted_iota(jnp.int32, (seg_len, 2 * seg_len), 1)
-    allowed = jnp.where(col_pos < seg_len, ctx_rank > 0, col_pos - seg_len <= row_pos)
-    scores = jnp.where(allowed[None], scores, NEG_FILL)
-    top_score = jnp.max(scores, axis=2, keepdims=True)
-    raised = jnp.exp(scores - top_score)
-    weights = (raised / jnp.sum(raised, axis=2, keepdims=True)).astype(BF16)
-    context = jnp.einsum("hqk,khe->qhe", weights, value_heads, preferred_element_type=F32)
-    context = context.astype(BF16).reshape(seg_len, heads_local * HD)
-    gain_out = lax.dynamic_slice_in_dim(head_gain, tp_rank * local_width, local_width)
-    hidden_out, own_bands = reduced_bands(
-        context, w_out, hidden_in, gain_out[None], proj_head, proj_middle, proj_tail
-    )
-    losses = band_losses(
-        own_bands, targets, clusters, (table_head, table_middle, table_tail)
-    )
-    return (hidden_out, losses)
+    tp_count = lax.axis_size("tp")
+    line = lax.axis_size("ctx") // 2
+    chips = tp_count // 2
+    tokens, width = hidden_in.shape
+    model_width = width * tp_count
+    rows = tokens // tp_count
+    bands = proj_head.shape[1] + proj_middle.shape[1] + proj_tail.shape[1]
+    goals = jnp.broadcast_to(targets[None], (8, tokens))
+    dma = pltpu.SemaphoreType.DMA
+    large = (w_query, w_key, w_value, w_out, proj_head, proj_middle, proj_tail)
+    tables = (table_head, table_middle, table_tail)
+    vmem = pl.BlockSpec(memory_space=pltpu.VMEM)
+    hidden_out, losses = pl.pallas_call(
+        functools.partial(layer_kernel, line, tp_count),
+        out_shape=(
+            jax.ShapeDtypeStruct((tokens, width), BF16),
+            jax.ShapeDtypeStruct((1, tokens), F32),
+        ),
+        in_specs=[vmem] * 5 + [pl.BlockSpec(memory_space=pl.ANY)] * 10,
+        out_specs=(vmem, vmem),
+        scratch_shapes=[pltpu.VMEM(a.shape, BF16) for a in large]
+        + [pltpu.VMEM(a.shape, BF16) for a in tables for _ in range(2)]
+        + [
+            pltpu.VMEM((2, tokens, model_width), BF16),
+            pltpu.VMEM((tokens, model_width), BF16),
+            pltpu.VMEM((tokens, width), BF16),
+            pltpu.VMEM((2 * tokens, width), BF16),
+            pltpu.VMEM((2 * tokens, width), BF16),
+            pltpu.VMEM((tokens, width), F32),
+            pltpu.VMEM((tokens, width), BF16),
+            pltpu.VMEM((rows, bands), BF16),
+        ]
+        + [pltpu.VMEM((chips, tokens, width), BF16)] * 4
+        + [pltpu.VMEM((tokens, bands), BF16)]
+        + [pltpu.VMEM((chips, rows, bands), BF16)] * 3
+        + [pltpu.VMEM((tokens, 128), F32), pltpu.VMEM((tp_count, rows, 128), F32)]
+        + [
+            pltpu.VMEM((line, tokens, bands), BF16),
+            pltpu.VMEM((line, 8, tokens), jnp.int32),
+            pltpu.VMEM((line, 8, tokens), F32),
+            pltpu.VMEM((line * tp_count, 8, tokens), F32),
+        ]
+        + [dma((10,)), dma((2, 3))]
+        + [dma((2,)), dma((2, 2, chips)), dma((2, 2, chips))]
+        + [dma((2, chips))] * 4
+        + [dma((2, tp_count))]
+        + [
+            dma((2, line + 1)),
+            dma((2, line + 1)),
+            dma((2, line, chips)),
+            dma((2, line, chips)),
+            dma((2, line)),
+            dma((2, line, tp_count)),
+        ],
+        compiler_params=pltpu.CompilerParams(
+            collective_id=0, has_side_effects=True, vmem_limit_bytes=62 * 1024 * 1024
+        ),
+    )(
+        hidden_in,
+        norm_gain[None],
+        head_gain[None],
+        clusters,
+        goals,
+        *large,
+        *tables,
+    )
+    return (hidden_out, losses[0])
 
 
 def solution(mesh):

time: 165 us -> 119 us (0.72)
  Pallas kernels: 80.3 us -> 114 us
  matrix products: 25.7 us -> 0 us
  waiting for transfers between devices: 20.9 us -> 0 us
  between operations: 14.3 us -> 0.64 us
  starting transfers between devices: 8.56 us -> 0 us
  local copies, waits for them, and re-layouts: 10.8 us -> 4.24 us
  other arithmetic: 3.98 us -> 0 us
    pallas_call x2 -> x1, Pallas kernels: 80.3 us -> 114 us  [body(): pl.pallas_call(functools.partial(layer_kernel, line, tp_count), out_shape...]
    dot_general x6 -> x0, matrix products: 22.1 us -> none  [the longest x5 17.9 us: project(): return jnp.dot(full_rows, weight, preferred_element_type=F32).astype(BF16)]
    all_gather x2 -> x0, waiting for transfers between devices: 16.2 us -> none  [the longest x1 8.44 us: body(): lax.all_gather(hidden_in, 'tp', axis=1, tiled=True)]
    ppermute x4 -> x0, starting transfers between devices: 8.49 us -> none  [the longest x1 4.87 us: body(): lax.ppermute(hidden_in, 'ctx', [(i, i + 1) for i in range(ctx_count - 1)])]
    ppermute x4 -> x0, waiting for transfers between devices: 4.08 us -> none  [the longest x1 4.07 us: body(): lax.ppermute(hidden_in, 'ctx', [(i, i + 1) for i in range(ctx_count - 1)])]
    reduce_sum x2 -> x0, other arithmetic: 3.74 us -> none  [norm_full(): mean_sq = jnp.mean(wide * wide, axis=1, keepdims=True)]
    sub x1 -> x0, matrix products: 3.62 us -> none  [body(): raised = jnp.exp(scores - top_score)]
    unnamed x30 -> x2, local copies, waits for them, and re-layouts: 5.15 us -> 2.96 us
  transfers between devices with their start and end apart: 6 -> 0, of which waited for: 3 -> 0; matrix products, arithmetic and copies ran while one was open for 21% -> 0% of each run, Pallas kernels for 18% -> 0%
where the time goes in v3:
time: 119 us
  Pallas kernels  114 us (96%)
  local copies, waits for them, and re-layouts  4.24 us (4%)
    pallas_call x1, Pallas kernels, body(): pl.pallas_call(functools.partial(layer_kernel, line, tp_count), out_shape...  114 us
    unnamed x2, local copies, waits for them, and re-layouts  2.96 us

profile of v3, /device:TPU:0, one launch (start us, length us, event | category | flops | bytes accessed | tf_op | source)
XLA Modules:
  0.0 118.6 jit_solution(5242939810711410331)
XLA Ops:
  0.6 1.3 %broadcast_in_dim.14.refs_4_ = s32[8,256]{1,0:T(8,128)} broadcast(s32[256]{0:T(256)} %param.29), dimensions={1} | broadcast | bytes 9216 | tf_op jit(solution)/shard_map/broadcast_in_dim | solution.py:741
  1.9 113.7 %shard_map.158 = (bf16[256,768]{1,0:T(8,128)(2,1)}, f32[1,256]{1,0:T(1,128)}) custom-call(bf16[256,768]{1,0:T(8,128)(2,1)} %refs_0_.1, f32[1,3072]{1,0:T(1,128)} %bitcast.3, f32[1,3072]{1,0:T(1,128)} %bitcast.4, bf16[2,2048]{1,0:T(2,128)(2,1)} %refs_3_.1, s32[8,256]{1,0:T(8,128)} %broadcast_in_dim.14.refs_4_, bf16[3072,768]{1,0:T(8,128)(2,1)} %refs_5_.1, ...), custom_call_target="tpu_custom_call" | custom-call | tf_op jit(solution)/shard_map/pallas_call | solution.py:746
  115.6 1.8 %copy.19 = bf16[256,768]{1,0:T(8,128)(2,1)} copy(bf16[256,768]{1,0:T(8,128)(2,1)} %get-tuple-element.8) | data formatting | bytes 786432
  117.4 1.2 %copy.20 = f32[256]{0:T(256)} copy(f32[256]{0:T(256)} %bitcast.5) | data formatting | bytes 2048

commit v4 on v3

--- a/solution.py
+++ b/solution.py
@@ -82,6 +82,7 @@
     buffers,
     sems,
     loads,
+    attend,
 ):
     a_send, a_recv, b_send, b_recv, part, c_recv, d_send, d_recv, sq_part, sq_recv = buffers
     a_sems, b_sems, c_sems, d_sems, sq_sems = sems
@@ -99,44 +100,82 @@
     def tokens(rank):
         return pl.ds(pl.multiple_of(rank * rows, rows), rows)
 
-    loads[0].wait()
-    context = context_ref[...]
     order = list(range(1, chips)) + [0]
     pending = []
-    acc = None
-    for j in order:
-        there = (chip + j) % chips
-        a_send[j] = jnp.dot(
-            context, w_out_ref[:, columns(there * 2 + 1 - core)], preferred_element_type=F32
-        ).astype(BF16)
-        copy = remote(a_send.at[j], a_recv.at[j], a_sems.at[0, j], a_sems.at[1, j], partner)
-        copy.start()
-        pending.append(copy)
-        mine = jnp.dot(
-            context, w_out_ref[:, columns(there * 2 + core)], preferred_element_type=F32
-        )
-        copy.wait_recv()
-        mine = mine + a_recv[j].astype(F32)
-        if j > 0:
-            b_send[j] = mine.astype(BF16)
-            copy = remote(
-                b_send.at[j],
-                b_recv.at[j],
-                b_sems.at[0, j],
-                b_sems.at[1, j],
-                tp_device(there * 2 + core),
-            )
+    kept = []
+    half_len = hidden_ref.shape[0] // 2
+
+    def lines(half):
+        return pl.ds(half * half_len, half_len)
+
+    def core_copy(j, half):
+        return remote(
+            a_send.at[j, lines(half), :],
+            a_recv.at[j, lines(half), :],
+            a_sems.at[0, j, half],
+            a_sems.at[1, j, half],
+            partner,
+        )
+
+    def chip_copy(j, half):
+        return remote(
+            b_send.at[j, lines(half), :],
+            b_recv.at[j, lines(half), :],
+            b_sems.at[0, j, half],
+            b_sems.at[1, j, half],
+            tp_device(((chip + j) % chips) * 2 + core),
+        )
+
+    for half in range(2):
+        attend(half)
+        if half == 0:
+            loads[0].wait()
+        context = context_ref[lines(half), :]
+        for j in order:
+            there = (chip + j) % chips
+            a_send[j, lines(half), :] = jnp.dot(
+                context, w_out_ref[:, columns(there * 2 + 1 - core)], preferred_element_type=F32
+            ).astype(BF16)
+            copy = core_copy(j, half)
             copy.start()
             pending.append(copy)
-        else:
-            acc = mine
-    for j in range(1, chips):
-        remote(b_send.at[j], b_recv.at[j], b_sems.at[0, j], b_sems.at[1, j], partner).wait_recv()
-        acc = acc + b_recv[j].astype(F32)
-    summed = hidden_ref[...].astype(F32) + acc
-    hidden_out_ref[...] = summed.astype(BF16)
-    squares = jnp.sum(summed * summed, 1, keepdims=True)
-    sq_part[...] = jnp.broadcast_to(squares, sq_part.shape)
+            mine = jnp.dot(
+                context, w_out_ref[:, columns(there * 2 + core)], preferred_element_type=F32
+            )
+            if j > 0:
+                copy.wait_recv()
+                b_send[j, lines(half), :] = (
+                    mine + a_recv[j, lines(half), :].astype(F32)
+                ).astype(BF16)
+                copy = chip_copy(j, half)
+                copy.start()
+                pending.append(copy)
+            else:
+                kept.append(mine)
+    for load in loads[1:]:
+        load.wait()
+    first = proj_head_ref.shape[1]
+    second = first + proj_middle_ref.shape[1]
+    for half in range(2):
+        core_copy(0, half).wait_recv()
+        acc = kept[half] + a_recv[0, lines(half), :].astype(F32)
+        for j in range(1, chips):
+            chip_copy(j, half).wait_recv()
+            acc = acc + b_recv[j, lines(half), :].astype(F32)
+        summed = hidden_ref[lines(half), :].astype(F32) + acc
+        hidden_out_ref[lines(half), :] = summed.astype(BF16)
+        squares = jnp.sum(summed * summed, 1, keepdims=True)
+        sq_part[lines(half), :] = jnp.broadcast_to(squares, (half_len, sq_part.shape[1]))
+        scaled = (summed * gain_ref[:, columns(tp)]).astype(BF16)
+        part[lines(half), :first] = jnp.dot(
+            scaled, proj_head_ref[...], preferred_element_type=F32
+        ).astype(BF16)
+        part[lines(half), first:second] = jnp.dot(
+            scaled, proj_middle_ref[...], preferred_element_type=F32
+        ).astype(BF16)
+        part[lines(half), second:] = jnp.dot(
+            scaled, proj_tail_ref[...], preferred_element_type=F32
+        ).astype(BF16)
     for step in range(1, tp_count):
         there = (tp + step) % tp_count
         copy = remote(
@@ -149,16 +188,6 @@
         copy.start()
         pending.append(copy)
 
-    scaled = (summed * gain_ref[:, columns(tp)]).astype(BF16)
-    for load in loads[1:]:
-        load.wait()
-    first = proj_head_ref.shape[1]
-    second = first + proj_middle_ref.shape[1]
-    part[:, :first] = jnp.dot(scaled, proj_head_ref[...], preferred_element_type=F32).astype(BF16)
-    part[:, first:second] = jnp.dot(
-        scaled, proj_middle_ref[...], preferred_element_type=F32
-    ).astype(BF16)
-    part[:, second:] = jnp.dot(scaled, proj_tail_ref[...], preferred_element_type=F32).astype(BF16)
     for j in order:
         there = (chip + j) % chips
         copy = remote(
@@ -235,7 +264,7 @@
     loads,
     swaps,
 ):
-    head_ref, head_pair_ref, middle_ref, middle_pair_ref, tail_ref, tail_pair_ref = table_refs
+    head_ref, middle_ref = table_refs[0], table_refs[2]
     bands, goals, stat_send, stat_recv = buffers
     z_send, z_recv, y_sems, c_sems, g_sems, s_sems = sems
     chips = tp_count // 2
@@ -312,7 +341,7 @@
         )
 
     bands[spot, pl.ds(pl.multiple_of(tp * rows, rows), rows), :] = own_ref[...]
-    goals[spot] = targets_ref[...]
+    goals[spot] = jnp.broadcast_to(targets_ref[...], goals.shape[1:])
 
     @pl.when(spot + 1 < line)
     def _():
@@ -325,16 +354,6 @@
     spread(spot)
     for k in range(1, line):
         goal_copy(k).start()
-    for k in range(1, line):
-        place = (spot - k + line) % line
-        remote(
-            goals.at[place], goals.at[place], g_sems.at[0, k], g_sems.at[1, k], device(spot, tp)
-        ).wait_recv()
-
-    for load in loads:
-        load.wait()
-    for swap in swaps:
-        swap.wait()
     place_own = tp * ctx_count + ctx
     place_pair = tp * ctx_count + spot * 2 + 1 - side
     first = head_ref.shape[1]
@@ -348,17 +367,27 @@
             across(source, j, 1 - core).wait_recv()
         goal = goals[source][0:1, :]
 
-        def band(low, high, base, own, pair):
-            size = own.shape[0]
-            piece = bands[source, :, low:high]
-            return combined(
-                band_stats(piece, own, goal - base - place_own * size),
-                band_stats(piece, pair, goal - base - place_pair * size),
+        limits = (0, first, second, bands.shape[2])
+        bases = (0, v0, v0 + v1)
+
+        def found_in(i, table, place):
+            return band_stats(
+                bands[source, :, limits[i] : limits[i + 1]],
+                table,
+                goal - bases[i] - place * table.shape[0],
             )
 
-        one = band(0, first, 0, head_ref, head_pair_ref)
-        two = band(first, second, v0, middle_ref, middle_pair_ref)
-        three = band(second, bands.shape[2], v0 + v1, tail_ref, tail_pair_ref)
+        own_found = [found_in(i, table_refs[2 * i], place_own) for i in range(3)]
+
+        @pl.when(source == spot)
+        def _():
+            for swap in swaps:
+                swap.wait()
+
+        one, two, three = [
+            combined(own_found[i], found_in(i, table_refs[2 * i + 1], place_pair))
+            for i in range(3)
+        ]
         found = (one[0], one[1], two[0], two[1], three[0], three[1], one[2] + two[2] + three[2])
         for i, value in enumerate(found):
             stat_send[source, i : i + 1, :] = value
@@ -370,7 +399,7 @@
         def _():
             stat_copy(source, 0).start()
 
-    def step(d, carry):
+    def pass_on(d):
         @pl.when((d + 1 < line) & (spot - d - 1 >= 0))
         def _():
             source = spot - d - 1
@@ -393,6 +422,11 @@
 
             spread(source)
 
+    def step(d, carry):
+        @pl.when(d > 0)
+        def _():
+            pass_on(d)
+
         @pl.when(spot - d >= 0)
         def _():
             finish(spot - d)
@@ -403,6 +437,15 @@
 
         return carry
 
+    pass_on(0)
+    for k in range(1, line):
+        place = (spot - k + line) % line
+        remote(
+            goals.at[place], goals.at[place], g_sems.at[0, k], g_sems.at[1, k], device(spot, tp)
+        ).wait_recv()
+
+    for load in loads:
+        load.wait()
     lax.fori_loop(0, line, step, 0)
 
     stat_recv[spot * tp_count + tp] = stat_send[spot]
@@ -570,38 +613,54 @@
     project(weights[1], keys, 0)
     project(weights[2], values, 0)
 
-    def heads(i, carry):
-        for h in range(4):
-            low = h * HD // 128 * 128
-            high = -(-(h + 1) * HD // 128) * 128
-            cut = pl.ds(pl.multiple_of(i * group + low, 128), high - low)
-            lane = lax.broadcasted_iota(jnp.int32, (seg_len, high - low), 1) + low
-            inside = (lane >= h * HD) & (lane < (h + 1) * HD)
-            query = jnp.where(inside, queries[:, cut].astype(F32), 0.0).astype(BF16)
-            scores = lax.dot_general(
-                query, keys[:, cut], (((1,), (1,)), ((), ())), preferred_element_type=F32
-            ) * HD ** (-0.5)
-            row_pos = lax.broadcasted_iota(jnp.int32, scores.shape, 0)
-            col_pos = lax.broadcasted_iota(jnp.int32, scores.shape, 1)
-            first = jnp.where(ctx > 0, 0, seg_len)
-            allowed = (col_pos >= first) & (col_pos - seg_len <= row_pos)
-            scores = jnp.where(allowed, scores, NEG_FILL)
-            raised = jnp.exp(scores - jnp.max(scores, axis=1, keepdims=True))
-            shares = (raised / jnp.sum(raised, axis=1, keepdims=True)).astype(BF16)
-            mixed = jnp.dot(shares, values[:, cut], preferred_element_type=F32)
-            acc[:, cut] = jnp.where(inside, mixed, acc[:, cut])
-        return carry
-
+    half_len = seg_len // 2
     acc[...] = jnp.zeros_like(acc)
-    lax.fori_loop(0, width // group, heads, 0)
-    context_ref[...] = acc[...].astype(BF16)
-
-    forward.wait_send()
-    for part in range(2):
-        for j in range(1, chips):
-            sideways(part, j).wait_send()
-        for j in range(chips):
-            across(part, j, core).wait_send()
+
+    def attend(half):
+        start = half * half_len
+        span = seg_len + start + half_len
+
+        def heads(i, carry):
+            for h in range(4):
+                low = h * HD // 128 * 128
+                high = -(-(h + 1) * HD // 128) * 128
+                cut = pl.ds(pl.multiple_of(i * group + low, 128), high - low)
+                lane = lax.broadcasted_iota(jnp.int32, (half_len, high - low), 1) + low
+                inside = (lane >= h * HD) & (lane < (h + 1) * HD)
+                query = jnp.where(
+                    inside, queries[start : start + half_len, cut].astype(F32), 0.0
+                ).astype(BF16)
+                scores = lax.dot_general(
+                    query,
+                    keys[:span, cut],
+                    (((1,), (1,)), ((), ())),
+                    preferred_element_type=F32,
+                ) * HD ** (-0.5)
+                row_pos = lax.broadcasted_iota(jnp.int32, scores.shape, 0) + start
+                col_pos = lax.broadcasted_iota(jnp.int32, scores.shape, 1)
+                first = jnp.where(ctx > 0, 0, seg_len)
+                allowed = (col_pos >= first) & (col_pos - seg_len <= row_pos)
+                scores = jnp.where(allowed, scores, NEG_FILL)
+                raised = jnp.exp(scores - jnp.max(scores, axis=1, keepdims=True))
+                shares = (raised / jnp.sum(raised, axis=1, keepdims=True)).astype(BF16)
+                mixed = jnp.dot(shares, values[:span, cut], preferred_element_type=F32)
+                acc[start : start + half_len, cut] = jnp.where(
+                    inside, mixed, acc[start : start + half_len, cut]
+                )
+            return carry
+
+        lax.fori_loop(0, width // group, heads, 0)
+        context_ref[start : start + half_len, :] = acc[start : start + half_len, :].astype(BF16)
+
+    def settle():
+        forward.wait_send()
+        for part in range(2):
+            for j in range(1, chips):
+                sideways(part, j).wait_send()
+            for j in range(chips):
+                across(part, j, core).wait_send()
+
+    return attend, settle
 
 
 def layer_kernel(line, tp_count, *refs):
@@ -674,7 +733,7 @@
         )
         for i, source in enumerate((th_ref, tm_ref, tt_ref))
     ]
-    attention_phase(
+    attend, settle = attention_phase(
         tp_count,
         ctx_count,
         hidden_ref,
@@ -698,6 +757,7 @@
         reduce,
         reduce_sems,
         loads[3:7],
+        attend,
     )
     loss_phase(
         line,
@@ -712,6 +772,7 @@
         loads[7:],
         swaps,
     )
+    settle()
 
 
 def body(
@@ -738,7 +799,6 @@
     model_width = width * tp_count
     rows = tokens // tp_count
     bands = proj_head.shape[1] + proj_middle.shape[1] + proj_tail.shape[1]
-    goals = jnp.broadcast_to(targets[None], (8, tokens))
     dma = pltpu.SemaphoreType.DMA
     large = (w_query, w_key, w_value, w_out, proj_head, proj_middle, proj_tail)
     tables = (table_head, table_middle, table_tail)
@@ -775,7 +835,8 @@
         ]
         + [dma((10,)), dma((2, 3))]
         + [dma((2,)), dma((2, 2, chips)), dma((2, 2, chips))]
-        + [dma((2, chips))] * 4
+        + [dma((2, chips, 2))] * 2
+        + [dma((2, chips))] * 2
         + [dma((2, tp_count))]
         + [
             dma((2, line + 1)),
@@ -793,7 +854,7 @@
         norm_gain[None],
         head_gain[None],
         clusters,
-        goals,
+        targets[None],
         *large,
         *tables,
     )

time: 119 us -> 112 us (0.941)
  Pallas kernels: 114 us -> 108 us
  local copies, waits for them, and re-layouts: 4.24 us -> 2.96 us
    pallas_call x1, Pallas kernels: 114 us -> 108 us  [body(): pl.pallas_call(functools.partial(layer_kernel, line, tp_count), out_shape...]
    broadcast_in_dim x1 -> x0, local copies, waits for them, and re-layouts: 1.28 us -> none  [body(): goals = jnp.broadcast_to(targets[None], (8, tokens))]
where the time goes in v4:
time: 112 us
  Pallas kernels  108 us (96%)
  local copies, waits for them, and re-layouts  2.96 us (3%)
    pallas_call x1, Pallas kernels, body(): pl.pallas_call(functools.partial(layer_kernel, line, tp_count), out_shape...  108 us
    unnamed x2, local copies, waits for them, and re-layouts  2.96 us

profile of v4, /device:TPU:0, one launch (start us, length us, event | category | flops | bytes accessed | tf_op | source)
XLA Modules:
  0.0 111.9 jit_solution(861463649664898938)
XLA Ops:
  0.6 108.3 %shard_map.158 = (bf16[256,768]{1,0:T(8,128)(2,1)}, f32[1,256]{1,0:T(1,128)}) custom-call(bf16[256,768]{1,0:T(8,128)(2,1)} %refs_0_.1, f32[1,3072]{1,0:T(1,128)} %bitcast.4, f32[1,3072]{1,0:T(1,128)} %bitcast.5, bf16[2,2048]{1,0:T(2,128)(2,1)} %refs_3_.1, s32[1,256]{1,0:T(1,128)} %bitcast.6, bf16[3072,768]{1,0:T(8,128)(2,1)} %refs_5_.1, ...), custom_call_target="tpu_custom_call" | custom-call | tf_op jit(solution)/shard_map/pallas_call | solution.py:806
  108.9 1.8 %copy.19 = bf16[256,768]{1,0:T(8,128)(2,1)} copy(bf16[256,768]{1,0:T(8,128)(2,1)} %get-tuple-element.8) | data formatting | bytes 786432
  110.7 1.2 %copy.20 = f32[256]{0:T(256)} copy(f32[256]{0:T(256)} %bitcast.7) | data formatting | bytes 2048
